TPU v7x, 256 devices: a whole 4x4x8 slice. The times are simulated.
256 devices in a mesh: cluster: 16 (over z, core), sub: 16 (over y, x).
Axes of the slice: x: 4, y: 4, z: 8, core: 2. Of those that a mesh axis runs over, the one named last changes fastest.
Arguments:
- dual_ops: bfloat16 [16, 16, 2048, 2048], P('cluster', 'sub'), as said below
- local_load: float32 [16, 16, 2048, 128], P('cluster', 'sub'), may hold values from -6 to 6
- rigid_modes: float32 [16, 16, 6, 2048], P('cluster', 'sub'), may hold values from -0.044194174 to 0.044194174, as said below
- coarse_load: float32 [16, 6, 128], P('cluster'), may hold values from -6 to 6
- gluing_peer: int32 [16, 16, 16], P('cluster', 'sub'), may hold values from 0 to 3, as said below
- gluing_sign: int32 [16, 16, 16], P('cluster', 'sub'), may hold values from -1 to 1, as said below
Outputs:
- multipliers: float32 [16, 16, 2048, 128], P('cluster', 'sub')
- amplitudes: float32 [16, 6, 128], P('cluster')
Inputs may be any that keep to these rules, and one draw needn't show every extreme that they name: `gluing_peer`: gluing is consistent: if block 4 k + f of subdomain t names peer j, the neighbour's block 4 j + (f xor 1) names k back; the map is one to one between facing blocks of two neighbours. Entries for missing neighbours are still in range. `gluing_sign`: every entry is -1 or 1; the two glued blocks of a neighbour pair carry opposite signs. `dual_ops`: each local dual operator is symmetric positive definite. `rigid_modes`: two glued blocks of neighbouring subdomains carry equal traces of every mode, entry by entry.
All inputs are finite; a program needn't handle non-finite values.
Results may differ from a plain program's by a relative error of at most 0.003.
Values sent between devices are 32-bit elements; how exact they have to be, the bound alone decides.
A program may use at most 64 MiB of HBM per device.

v0:
```python
import jax
import jax.numpy as jnp
from jax import lax
from jax.sharding import PartitionSpec as P

ITERS = 2


HIGHEST = lax.Precision.HIGHEST


def passed_along(value, axis, steps):
    count = lax.axis_size(axis)
    leading, last = (max(0, -steps), min(count, count - steps))
    return lax.ppermute(value, axis, [(source, source + steps) for source in range(leading, last)])


def per_device(dual_ops, local_load, rigid_modes, coarse_load, gluing_peer, gluing_sign):
    operator = dual_ops[0, 0]
    mode_rows = rigid_modes[0, 0]
    dual_size = operator.shape[0]
    block_rows = dual_size // 16
    mode_count = mode_rows.shape[0]
    load_count = local_load.shape[-1]
    cluster_count = lax.axis_size("cluster")
    sub_count = lax.axis_size("sub")
    cluster_index = lax.axis_index("cluster")
    sub_index = lax.axis_index("sub")
    peer_table = gluing_peer[0, 0].reshape(4, 4)
    sign_field = jnp.repeat(gluing_sign[0, 0].astype(jnp.float32), block_rows)[:, None]
    has_peer = jnp.stack(
        [
            sub_index > 0,
            sub_index < sub_count - 1,
            cluster_index > 0,
            cluster_index < cluster_count - 1,
        ]
    )
    block_weight = jnp.where(has_peer, 0.5, 1.0).astype(jnp.float32)
    weights = jnp.broadcast_to(block_weight[None, :, None], (4, 4, block_rows)).reshape(
        dual_size, 1
    )

    def neighbour_parts(local_part):
        breadth = local_part.shape[-1]
        shaped = local_part.reshape(4, 4, block_rows, breadth)
        incoming = (
            passed_along(shaped[:, 1], "sub", 1),
            passed_along(shaped[:, 0], "sub", -1),
            passed_along(shaped[:, 3], "cluster", 1),
            passed_along(shaped[:, 2], "cluster", -1),
        )
        return [
            jnp.take(arrived, peer_table[:, facing], axis=0)
            for facing, arrived in enumerate(incoming)
        ]

    def place(pieces, breadth):
        return jnp.stack(pieces, axis=1).reshape(dual_size, breadth)

    def assemble(local_part):
        return local_part + place(neighbour_parts(local_part), local_part.shape[-1])

    signed_modes = sign_field * mode_rows.T
    mode_pieces = neighbour_parts(signed_modes)
    zero_piece = jnp.zeros_like(mode_pieces[0])
    own_columns = signed_modes + place(
        [mode_pieces[0], mode_pieces[1], zero_piece, zero_piece], mode_count
    )
    lower_columns = place([zero_piece, zero_piece, mode_pieces[2], zero_piece], mode_count)
    upper_columns = place([zero_piece, zero_piece, zero_piece, mode_pieces[3]], mode_count)
    stacked = jnp.stack([own_columns, lower_columns, upper_columns])
    row_terms = jnp.einsum("km,jmn->jkn", mode_rows, sign_field[None] * stacked, precision=HIGHEST)
    cluster_rows = lax.psum(row_terms, "sub")
    all_rows = lax.all_gather(cluster_rows[None], "cluster", axis=0, tiled=True)
    cluster_ids = jnp.arange(cluster_count)
    adjacency = jnp.stack(
        [
            cluster_ids[None, :] == cluster_ids[:, None],
            cluster_ids[None, :] == cluster_ids[:, None] - 1,
            cluster_ids[None, :] == cluster_ids[:, None] + 1,
        ]
    ).astype(jnp.float32)
    coarse = jnp.einsum("jcd,cjkn->ckdn", adjacency, all_rows, precision=HIGHEST)
    coarse = coarse.reshape(cluster_count * mode_count, cluster_count * mode_count)
    factor = jnp.linalg.cholesky(coarse)

    def solve(right_side):
        return jax.scipy.linalg.cho_solve((factor, True), right_side)

    def spread(amplitudes):
        blocks = amplitudes.reshape(cluster_count, mode_count, -1)
        current = lax.dynamic_index_in_dim(blocks, cluster_index, 0, keepdims=False)
        return assemble(sign_field * jnp.dot(mode_rows.T, current, precision=HIGHEST))

    def restrict(field):
        return jnp.dot(mode_rows, sign_field * field, precision=HIGHEST)

    def project(residual):
        local_terms = restrict(residual)
        cluster_terms = lax.psum(local_terms, "sub")
        gathered = lax.all_gather(cluster_terms, "cluster", axis=0, tiled=True)
        amplitudes = solve(gathered)
        projected = residual - spread(amplitudes)
        norm_value = lax.psum(jnp.sum(weights * projected * projected, axis=0), ("cluster", "sub"))
        total_squares = norm_value + jnp.sum(gathered * amplitudes, axis=0)
        return (projected, norm_value, amplitudes, gathered, total_squares)

    def dual_images(direction):
        signed = (sign_field * direction).astype(jnp.bfloat16)
        images = jnp.dot(operator, signed, preferred_element_type=jnp.float32)
        return (signed, images, assemble(sign_field * images))

    all_loads = lax.all_gather(coarse_load, "cluster", axis=0, tiled=True)
    dual_load = assemble(sign_field * local_load[0, 0])
    start_amplitudes = solve(all_loads.reshape(cluster_count * mode_count, load_count))
    multipliers = spread(start_amplitudes)
    residual = dual_load - dual_images(multipliers)[2]
    projected, norm_now, amplitudes, gathered, total_squares = project(residual)
    direction = projected
    for step_index in range(ITERS):
        signed, images, image = dual_images(direction)
        curvature_terms = jnp.sum(signed.astype(jnp.float32) * images, axis=0)
        curvature = lax.psum(curvature_terms, ("cluster", "sub"))
        length = norm_now / curvature
        multipliers = multipliers + length * direction
        residual = residual - length * image
        projected, norm_next, amplitudes, gathered, total_squares = project(residual)
        direction = projected + norm_next / norm_now * direction
        norm_now = norm_next
    own_amplitudes = lax.dynamic_slice_in_dim(
        amplitudes.reshape(cluster_count, mode_count, load_count), cluster_index, 1, 0
    )
    return (multipliers[None, None], own_amplitudes)


def solution(mesh):
    return jax.shard_map(
        per_device,
        mesh=mesh,
        in_specs=(
            P("cluster", "sub", None, None),
            P("cluster", "sub", None, None),
            P("cluster", "sub", None, None),
            P("cluster", None, None),
            P("cluster", "sub", None),
            P("cluster", "sub", None),
        ),
        out_specs=(P("cluster", "sub", None, None), P("cluster", None, None)),
        check_vma=False,
    )
```

profile of v0, /device:TPU:1, one launch (start us, length us, event | category | flops | bytes accessed | tf_op | source)
XLA Modules:
  0.0 808.4 jit_solution(15213485754353475690)
XLA Ops:
  2.4 4.9 collective-permute-start.2
  7.3 1.9 collective-permute-start.3
  10.6 4.0 collective-permute-start
  18.4 20.7 %all_gather.16 = f32[16,6,128]{2,1,0:T(8,128)S(1)} all-gather(f32[1,6,128]{2,1,0:T(8,128)S(1)} %copy.120), channel_id=1, replica_groups=mesh['cluster'=16,'sub'=16] {'cluster'}, dimensions={0}, use_global_device_ids=true | all-gather | bytes 52224 | tf_op jit(solution)/shard_map/all_gather | solution.py:114
  44.4 58.8 %psum.56 = f32[1,3,6,6]{3,2,1,0:T(8,128)S(1)} all-reduce(f32[1,3,6,6]{3,2,1,0:T(8,128)S(1)} %bitcast.303), channel_id=1, replica_groups=mesh['cluster'=16,'sub'=16] {'sub'}, use_global_device_ids=true, to_apply=%region_0.2 | all-reduce | flops 108 | bytes 864 | tf_op jit(solution)/shard_map/psum | solution.py:74
  103.2 29.6 %all_gather.15 = f32[16,3,6,6]{3,2,1,0:T(8,128)S(1)} all-gather(f32[1,3,6,6]{3,2,1,0:T(8,128)S(1)} %psum.56), channel_id=1, replica_groups=mesh['cluster'=16,'sub'=16] {'cluster'}, dimensions={0}, use_global_device_ids=true | all-gather | bytes 7344 | tf_op jit(solution)/shard_map/all_gather | solution.py:75
  134.4 8.8 %cholesky.18 = f32[96,96]{1,0:T(8,128)S(1)} custom-call(f32[96,96]{1,0:T(8,128)S(1)} %fusion.61), custom_call_target="Cholesky" | custom-call | tf_op jit(solution)/shard_map/jit(cholesky)/cholesky | solution.py:86
  144.5 7.4 custom-call.11
  152.4 1.8 fusion.14
  158.3 2.1 collective-permute-start.7
  161.6 3.5 collective-permute-start.6
  166.1 1.9 collective-permute-start.11
  168.0 3.6 collective-permute-start.10
  177.1 4.6 collective-permute-start.4
  182.4 5.1 collective-permute-done.5
  187.6 2.2 collective-permute-start.8
  193.4 6.4 fusion.18
  203.8 2.4 collective-permute-start.15
  206.3 1.8 copy.170
  208.1 3.1 collective-permute-start.14
  221.6 4.7 collective-permute-start.12
  238.6 2.6 reshape.233
  243.8 2.7 reshape.235
  246.4 1.9 fusion.24
  249.2 28.8 %psum.57 = f32[6,128]{1,0:T(8,128)S(1)} all-reduce(f32[6,128]{1,0:T(8,128)S(1)} %convolution_bitcast_fusion.4), channel_id=1, replica_groups=mesh['cluster'=16,'sub'=16] {'sub'}, use_global_device_ids=true, to_apply=%region_3.7 | all-reduce | flops 768 | bytes 6144 | tf_op jit(solution)/shard_map/psum | solution.py:101
  278.1 23.1 %all-gather = f32[16,6,128]{2,1,0:T(8,128)S(1)} all-gather(f32[1,6,128]{2,1,0:T(8,128)S(1)} %bitcast.308), channel_id=1, replica_groups=mesh['cluster'=16,'sub'=16] {'cluster'}, dimensions={0}, use_global_device_ids=true | all-gather | bytes 52224 | tf_op jit(solution)/shard_map/all_gather | solution.py:102
  306.2 2.1 collective-permute-start.19
  310.0 3.5 collective-permute-start.18
  318.0 4.0 collective-permute-start.16
  331.3 2.7 reshape.238
  335.4 6.9 multiply_reduce_fusion.1
  344.1 4.6 fusion.79
  350.5 2.0 collective-permute-start.23
  352.4 1.8 copy.178
  354.2 3.6 collective-permute-start.22
  361.7 5.0 collective-permute-start.20
  366.8 74.8 %all-reduce = (f32[128]{0:T(128)S(1)}, f32[128]{0:T(128)S(1)}) all-reduce(f32[128]{0:T(128)} %get-tuple-element.14, f32[128]{0:T(128)} %get-tuple-element.13), channel_id=1, replica_groups=mesh['cluster'=16,'sub'=16] {'cluster','sub'}, use_global_device_ids=true, to_apply=%region_5.9 | all-reduce | flops 256 | bytes 2048 | tf_op jit(solution)/shard_map/psum | solution.py:105
  450.7 2.2 pad_maximum_fusion.4
  452.9 2.6 copy.144
  455.6 2.7 reshape.240
  460.9 30.7 %psum.60 = f32[6,128]{1,0:T(8,128)S(1)} all-reduce(f32[6,128]{1,0:T(8,128)S(1)} %convolution_bitcast_fusion.3), channel_id=1, replica_groups=mesh['cluster'=16,'sub'=16] {'sub'}, use_global_device_ids=true, to_apply=%region_8.12 | all-reduce | flops 768 | bytes 6144 | tf_op jit(solution)/shard_map/psum | solution.py:101
  491.5 22.7 %all-gather.1 = f32[16,6,128]{2,1,0:T(8,128)S(1)} all-gather(f32[1,6,128]{2,1,0:T(8,128)S(1)} %bitcast.309), channel_id=1, replica_groups=mesh['cluster'=16,'sub'=16] {'cluster'}, dimensions={0}, use_global_device_ids=true | all-gather | bytes 52224 | tf_op jit(solution)/shard_map/all_gather | solution.py:102
  517.4 4.4 fusion.78
  523.6 2.1 collective-permute-start.27
  527.4 3.5 collective-permute-start.26
  534.8 4.7 collective-permute-start.24
  548.1 2.2 pad_maximum_fusion.5
  550.3 2.6 copy.149
  552.9 2.6 reshape.243
  555.5 2.4 fusion.22
  558.0 72.6 %psum.61 = f32[128]{0:T(128)S(1)} all-reduce(f32[128]{0:T(128)S(1)} %get-tuple-element.21), channel_id=1, replica_groups=mesh['cluster'=16,'sub'=16] {'cluster','sub'}, use_global_device_ids=true, to_apply=%region_10.14 | all-reduce | flops 128 | bytes 1024 | tf_op jit(solution)/shard_map/psum | solution.py:105
  631.3 8.3 %broadcast_multiply_fusion = (f32[2048,128]{0,1:T(8,128)}, f32[128]{0:T(128)S(1)}, f32[2048,128]{0,1:T(8,128)}) fusion(f32[2048]{0:T(1024)S(1)} %broadcast_bitcast_fusion, bf16[1,1,2048,2048]{3,2,1,0:T(8,128)(2,1)} %param.12, f32[2048,128]{0,1:T(8,128)} %get-tuple-element.22, f32[2048,128]{0,1:T(8,128)S(1)} %add_subtract_fusion.1, f32[128]{0:T(128)S(1)} %div.20), kind=kOutput, calls=%fused_computation.86 | convolution fusion | flops 1076887424 | bytes 12592128 | tf_op jit(solution)/shard_map/dot_general | solution.py:111
  639.6 73.7 %psum.62 = f32[128]{0:T(128)S(1)} all-reduce(f32[128]{0:T(128)S(1)} %get-tuple-element.29), channel_id=1, replica_groups=mesh['cluster'=16,'sub'=16] {'cluster','sub'}, use_global_device_ids=true, to_apply=%region_12.16 | all-reduce | flops 128 | bytes 1024 | tf_op jit(solution)/shard_map/psum | solution.py:124
  713.8 2.9 reshape.244
  716.8 4.6 fusion.77
  723.2 2.6 collective-permute-start.31
  725.7 1.8 copy.186
  727.6 3.0 collective-permute-start.30
  730.5 2.6 add_bitcast_fusion
  733.2 2.5 copy.155
  738.2 4.0 collective-permute-start.28
  749.3 2.3 convolution_bitcast_fusion.2
  751.6 31.6 %psum.63 = f32[6,128]{1,0:T(8,128)S(1)} all-reduce(f32[6,128]{1,0:T(8,128)S(1)} %convolution_bitcast_fusion.2), channel_id=1, replica_groups=mesh['cluster'=16,'sub'=16] {'sub'}, use_global_device_ids=true, to_apply=%region_13.17 | all-reduce | flops 768 | bytes 6144 | tf_op jit(solution)/shard_map/psum | solution.py:101
  783.2 24.0 %all-gather.2 = f32[16,6,128]{2,1,0:T(8,128)S(1)} all-gather(f32[1,6,128]{2,1,0:T(8,128)S(1)} %bitcast.310), channel_id=1, replica_groups=mesh['cluster'=16,'sub'=16] {'cluster'}, dimensions={0}, use_global_device_ids=true | all-gather | bytes 52224 | tf_op jit(solution)/shard_map/all_gather | solution.py:102
  (247 shorter events, 135.0 us)
Async XLA Ops:
  0.6 159.8 %copy-start.4 = (f32[1,1,2048,128]{3,2,1,0:T(8,128)S(1)}, f32[1,1,2048,128]{3,2,1,0:T(8,128)}, u32[]{:S(2)}) copy-start(f32[1,1,2048,128]{3,2,1,0:T(8,128)} %param.13) | copy-start | bytes 3145732
  2.4 36.9 %collective-permute-start.2 = (f32[4,128,6]{1,2,0:T(8,128)S(1)}, f32[4,128,6]{1,2,0:T(8,128)S(1)}, u32[]{:S(2)}, u32[]{:S(2)}) collective-permute-start(f32[4,128,6]{1,2,0:T(8,128)S(1)} %bitcast.307), channel_id=1, source_target_pairs={{0,16},{16,32},{32,48},{48,64},{64,80},{80,96},{96,112},{112,128},... | collective-permute-start | bytes 36872 | tf_op jit(solution)/shard_map/ppermute | solution.py:15
  7.3 32.6 %collective-permute-start.3 = (f32[4,128,6]{1,2,0:T(8,128)S(1)}, f32[4,128,6]{1,2,0:T(8,128)S(1)}, u32[]{:S(2)}, u32[]{:S(2)}) collective-permute-start(f32[4,128,6]{1,2,0:T(8,128)S(1)} %bitcast.306), channel_id=1, source_target_pairs={{16,0},{32,16},{48,32},{64,48},{80,64},{96,80},{112,96},{128,112},... | collective-permute-start | bytes 36872 | tf_op jit(solution)/shard_map/ppermute | solution.py:15
  9.3 31.3 %collective-permute-start.1 = (f32[4,128,6]{1,2,0:T(8,128)S(1)}, f32[4,128,6]{1,2,0:T(8,128)S(1)}, u32[]{:S(2)}, u32[]{:S(2)}) collective-permute-start(f32[4,128,6]{1,2,0:T(8,128)S(1)} %bitcast.305), channel_id=1, source_target_pairs={{1,0},{2,1},{3,2},{4,3},{5,4},{6,5},{7,6},{8,7},{9,8},{10,9},{11,1... | collective-permute-start | bytes 36872 | tf_op jit(solution)/shard_map/ppermute | solution.py:15
  10.6 30.7 %collective-permute-start = (f32[4,128,6]{1,2,0:T(8,128)S(1)}, f32[4,128,6]{1,2,0:T(8,128)S(1)}, u32[]{:S(2)}, u32[]{:S(2)}) collective-permute-start(f32[4,128,6]{1,2,0:T(8,128)S(1)} %bitcast.304), channel_id=1, source_target_pairs={{0,1},{1,2},{2,3},{3,4},{4,5},{5,6},{6,7},{7,8},{8,9},{9,10},{10,1... | collective-permute-start | bytes 36872 | tf_op jit(solution)/shard_map/ppermute | solution.py:15
  158.3 15.9 %collective-permute-start.7 = (f32[4,128,128]{2,1,0:T(8,128)}, f32[4,128,128]{2,1,0:T(8,128)}, u32[]{:S(2)}, u32[]{:S(2)}) collective-permute-start(f32[4,128,128]{2,1,0:T(8,128)} %bitcast.28), channel_id=1, source_target_pairs={{16,0},{32,16},{48,32},{64,48},{80,64},{96,80},{112,96},{128,112},... | collective-permute-start | bytes 786440 | tf_op jit(solution)/shard_map/ppermute | solution.py:15
  161.6 15.5 %collective-permute-start.6 = (f32[4,128,128]{2,1,0:T(8,128)S(1)}, f32[4,128,128]{2,1,0:T(8,128)S(1)}, u32[]{:S(2)}, u32[]{:S(2)}) collective-permute-start(f32[4,128,128]{2,1,0:T(8,128)S(1)} %bitcast.283), channel_id=1, source_target_pairs={{0,16},{16,32},{32,48},{48,64},{64,80},{80,96},{96,112},{112,128},... | collective-permute-start | bytes 786440 | tf_op jit(solution)/shard_map/ppermute | solution.py:15
  166.1 41.9 %collective-permute-start.11 = (f32[4,128,128]{2,1,0:T(8,128)}, f32[4,128,128]{2,1,0:T(8,128)}, u32[]{:S(2)}, u32[]{:S(2)}) collective-permute-start(f32[4,128,128]{2,1,0:T(8,128)} %get-tuple-element.47), channel_id=1, source_target_pairs={{16,0},{32,16},{48,32},{64,48},{80,64},{96,80},{112,96},{128,112},... | collective-permute-start | bytes 786440 | tf_op jit(solution)/shard_map/ppermute | solution.py:15
  168.0 45.0 %collective-permute-start.10 = (f32[4,128,128]{2,1,0:T(8,128)}, f32[4,128,128]{2,1,0:T(8,128)}, u32[]{:S(2)}, u32[]{:S(2)}) collective-permute-start(f32[4,128,128]{2,1,0:T(8,128)} %get-tuple-element.48), channel_id=1, source_target_pairs={{0,16},{16,32},{32,48},{48,64},{64,80},{80,96},{96,112},{112,128},... | collective-permute-start | bytes 786440 | tf_op jit(solution)/shard_map/ppermute | solution.py:15
  171.7 42.9 %collective-permute-start.9 = (f32[4,128,128]{2,1,0:T(8,128)}, f32[4,128,128]{2,1,0:T(8,128)}, u32[]{:S(2)}, u32[]{:S(2)}) collective-permute-start(f32[4,128,128]{2,1,0:T(8,128)} %get-tuple-element.49), channel_id=1, source_target_pairs={{1,0},{2,1},{3,2},{4,3},{5,4},{6,5},{7,6},{8,7},{9,8},{10,9},{11,1... | collective-permute-start | bytes 786440 | tf_op jit(solution)/shard_map/ppermute | solution.py:15
  174.2 13.4 %collective-permute-start.5 = (f32[4,128,128]{2,1,0:T(8,128)S(1)}, f32[4,128,128]{2,1,0:T(8,128)S(1)}, u32[]{:S(2)}, u32[]{:S(2)}) collective-permute-start(f32[4,128,128]{2,1,0:T(8,128)S(1)} %bitcast.297), channel_id=1, source_target_pairs={{1,0},{2,1},{3,2},{4,3},{5,4},{6,5},{7,6},{8,7},{9,8},{10,9},{11,1... | collective-permute-start | bytes 786440 | tf_op jit(solution)/shard_map/ppermute | solution.py:15
  177.1 13.3 %collective-permute-start.4 = (f32[4,128,128]{2,1,0:T(8,128)S(1)}, f32[4,128,128]{2,1,0:T(8,128)S(1)}, u32[]{:S(2)}, u32[]{:S(2)}) collective-permute-start(f32[4,128,128]{2,1,0:T(8,128)S(1)} %bitcast.284), channel_id=1, source_target_pairs={{0,1},{1,2},{2,3},{3,4},{4,5},{5,6},{6,7},{7,8},{8,9},{9,10},{10,1... | collective-permute-start | bytes 786440 | tf_op jit(solution)/shard_map/ppermute | solution.py:15
  187.6 28.5 %collective-permute-start.8 = (f32[4,128,128]{2,1,0:T(8,128)}, f32[4,128,128]{2,1,0:T(8,128)}, u32[]{:S(2)}, u32[]{:S(2)}) collective-permute-start(f32[4,128,128]{2,1,0:T(8,128)} %get-tuple-element.46), channel_id=1, source_target_pairs={{0,1},{1,2},{2,3},{3,4},{4,5},{5,6},{6,7},{7,8},{8,9},{9,10},{10,1... | collective-permute-start | bytes 786440 | tf_op jit(solution)/shard_map/ppermute | solution.py:15
  192.4 1.0 copy-start
  193.4 17.8 %copy-start.5 = (f32[1,1,2048,128]{3,2,1,0:T(8,128)S(1)}, f32[1,1,2048,128]{3,2,1,0:T(8,128)}, u32[]{:S(2)}) copy-start(f32[1,1,2048,128]{3,2,1,0:T(8,128)} %param.13) | copy-start | bytes 3145732
  203.8 22.4 %collective-permute-start.15 = (f32[4,128,128]{2,1,0:T(8,128)}, f32[4,128,128]{2,1,0:T(8,128)}, u32[]{:S(2)}, u32[]{:S(2)}) collective-permute-start(f32[4,128,128]{2,1,0:T(8,128)} %bitcast.53), channel_id=1, source_target_pairs={{16,0},{32,16},{48,32},{64,48},{80,64},{96,80},{112,96},{128,112},... | collective-permute-start | bytes 786440 | tf_op jit(solution)/shard_map/ppermute | solution.py:15
  208.1 20.6 %collective-permute-start.14 = (f32[4,128,128]{2,1,0:T(8,128)}, f32[4,128,128]{2,1,0:T(8,128)}, u32[]{:S(2)}, u32[]{:S(2)}) collective-permute-start(f32[4,128,128]{2,1,0:T(8,128)} %bitcast.51), channel_id=1, source_target_pairs={{0,16},{16,32},{32,48},{48,64},{64,80},{80,96},{96,112},{112,128},... | collective-permute-start | bytes 786440 | tf_op jit(solution)/shard_map/ppermute | solution.py:15
  219.4 11.7 %collective-permute-start.13 = (f32[4,128,128]{2,1,0:T(8,128)}, f32[4,128,128]{2,1,0:T(8,128)}, u32[]{:S(2)}, u32[]{:S(2)}) collective-permute-start(f32[4,128,128]{2,1,0:T(8,128)} %bitcast.291), channel_id=1, source_target_pairs={{1,0},{2,1},{3,2},{4,3},{5,4},{6,5},{7,6},{8,7},{9,8},{10,9},{11,1... | collective-permute-start | bytes 786440 | tf_op jit(solution)/shard_map/ppermute | solution.py:15
  221.6 12.0 %collective-permute-start.12 = (f32[4,128,128]{2,1,0:T(8,128)}, f32[4,128,128]{2,1,0:T(8,128)}, u32[]{:S(2)}, u32[]{:S(2)}) collective-permute-start(f32[4,128,128]{2,1,0:T(8,128)} %bitcast.285), channel_id=1, source_target_pairs={{0,1},{1,2},{2,3},{3,4},{4,5},{5,6},{6,7},{7,8},{8,9},{9,10},{10,1... | collective-permute-start | bytes 786440 | tf_op jit(solution)/shard_map/ppermute | solution.py:15
  228.7 12.5 %copy-start.6 = (f32[4,1,128,128]{3,2,0,1:T(8,128)S(1)}, f32[4,1,128,128]{3,2,0,1:T(8,128)}, u32[]{:S(2)}) copy-start(f32[4,1,128,128]{3,2,0,1:T(8,128)} %get-tuple-element.67) | copy-start | bytes 786436
  237.1 11.2 %copy-start.3 = (f32[1,1,6,2048]{3,1,2,0:T(1,128)S(1)}, f32[1,1,6,2048]{3,1,2,0:T(1,128)}, u32[]{:S(2)}) copy-start(f32[1,1,6,2048]{3,1,2,0:T(1,128)} %param.14) | copy-start | bytes 147460
  306.2 15.9 %collective-permute-start.19 = (f32[4,128,128]{2,1,0:T(8,128)S(1)}, f32[4,128,128]{2,1,0:T(8,128)S(1)}, u32[]{:S(2)}, u32[]{:S(2)}) collective-permute-start(f32[4,128,128]{2,1,0:T(8,128)S(1)} %bitcast.282), channel_id=1, source_target_pairs={{16,0},{32,16},{48,32},{64,48},{80,64},{96,80},{112,96},{128,112},... | collective-permute-start | bytes 786440 | tf_op jit(solution)/shard_map/ppermute | solution.py:15
  310.0 12.7 %collective-permute-start.18 = (f32[4,128,128]{2,1,0:T(8,128)}, f32[4,128,128]{2,1,0:T(8,128)S(1)}, u32[]{:S(2)}, u32[]{:S(2)}) collective-permute-start(f32[4,128,128]{2,1,0:T(8,128)} %bitcast.65), channel_id=1, source_target_pairs={{0,16},{16,32},{32,48},{48,64},{64,80},{80,96},{96,112},{112,128},... | collective-permute-start | bytes 786440 | tf_op jit(solution)/shard_map/ppermute | solution.py:15
  315.9 9.6 %collective-permute-start.17 = (f32[4,128,128]{2,1,0:T(8,128)}, f32[4,128,128]{2,1,0:T(8,128)}, u32[]{:S(2)}, u32[]{:S(2)}) collective-permute-start(f32[4,128,128]{2,1,0:T(8,128)} %bitcast.63), channel_id=1, source_target_pairs={{1,0},{2,1},{3,2},{4,3},{5,4},{6,5},{7,6},{8,7},{9,8},{10,9},{11,1... | collective-permute-start | bytes 786440 | tf_op jit(solution)/shard_map/ppermute | solution.py:15
  318.0 10.1 %collective-permute-start.16 = (f32[4,128,128]{2,1,0:T(8,128)}, f32[4,128,128]{2,1,0:T(8,128)S(1)}, u32[]{:S(2)}, u32[]{:S(2)}) collective-permute-start(f32[4,128,128]{2,1,0:T(8,128)} %bitcast.295), channel_id=1, source_target_pairs={{0,1},{1,2},{2,3},{3,4},{4,5},{5,6},{6,7},{7,8},{8,9},{9,10},{10,1... | collective-permute-start | bytes 786440 | tf_op jit(solution)/shard_map/ppermute | solution.py:15
  329.9 5.5 copy-start.8
  342.4 113.2 %copy-start.2 = (f32[2048,128]{0,1:T(8,128)}, f32[2048,128]{0,1:T(8,128)S(1)}, u32[]{:S(2)}) copy-start(f32[2048,128]{0,1:T(8,128)S(1)} %get-tuple-element.23) | copy-start | bytes 3145732
  350.5 91.7 %collective-permute-start.23 = (f32[4,128,128]{2,1,0:T(8,128)}, f32[4,128,128]{2,1,0:T(8,128)}, u32[]{:S(2)}, u32[]{:S(2)}) collective-permute-start(f32[4,128,128]{2,1,0:T(8,128)} %bitcast.292), channel_id=1, source_target_pairs={{16,0},{32,16},{48,32},{64,48},{80,64},{96,80},{112,96},{128,112},... | collective-permute-start | bytes 786440 | tf_op jit(solution)/shard_map/ppermute | solution.py:15
  354.2 90.2 %collective-permute-start.22 = (f32[4,128,128]{2,1,0:T(8,128)}, f32[4,128,128]{2,1,0:T(8,128)}, u32[]{:S(2)}, u32[]{:S(2)}) collective-permute-start(f32[4,128,128]{2,1,0:T(8,128)} %bitcast.289), channel_id=1, source_target_pairs={{0,16},{16,32},{32,48},{48,64},{64,80},{80,96},{96,112},{112,128},... | collective-permute-start | bytes 786440 | tf_op jit(solution)/shard_map/ppermute | solution.py:15
  359.6 87.2 %collective-permute-start.21 = (f32[4,128,128]{2,1,0:T(8,128)}, f32[4,128,128]{2,1,0:T(8,128)}, u32[]{:S(2)}, u32[]{:S(2)}) collective-permute-start(f32[4,128,128]{2,1,0:T(8,128)} %bitcast.287), channel_id=1, source_target_pairs={{1,0},{2,1},{3,2},{4,3},{5,4},{6,5},{7,6},{8,7},{9,8},{10,9},{11,1... | collective-permute-start | bytes 786440 | tf_op jit(solution)/shard_map/ppermute | solution.py:15
  361.7 87.4 %collective-permute-start.20 = (f32[4,128,128]{2,1,0:T(8,128)}, f32[4,128,128]{2,1,0:T(8,128)}, u32[]{:S(2)}, u32[]{:S(2)}) collective-permute-start(f32[4,128,128]{2,1,0:T(8,128)} %bitcast.286), channel_id=1, source_target_pairs={{0,1},{1,2},{2,3},{3,4},{4,5},{5,6},{6,7},{7,8},{8,9},{9,10},{10,1... | collective-permute-start | bytes 786440 | tf_op jit(solution)/shard_map/ppermute | solution.py:15
  441.6 0.6 copy-start.9
  523.6 15.9 %collective-permute-start.27 = (f32[4,128,128]{2,1,0:T(8,128)}, f32[4,128,128]{2,1,0:T(8,128)}, u32[]{:S(2)}, u32[]{:S(2)}) collective-permute-start(f32[4,128,128]{2,1,0:T(8,128)} %bitcast.300), channel_id=1, source_target_pairs={{16,0},{32,16},{48,32},{64,48},{80,64},{96,80},{112,96},{128,112},... | collective-permute-start | bytes 786440 | tf_op jit(solution)/shard_map/ppermute | solution.py:15
  527.4 14.4 %collective-permute-start.26 = (f32[4,128,128]{2,1,0:T(8,128)}, f32[4,128,128]{2,1,0:T(8,128)}, u32[]{:S(2)}, u32[]{:S(2)}) collective-permute-start(f32[4,128,128]{2,1,0:T(8,128)} %bitcast.299), channel_id=1, source_target_pairs={{0,16},{16,32},{32,48},{48,64},{64,80},{80,96},{96,112},{112,128},... | collective-permute-start | bytes 786440 | tf_op jit(solution)/shard_map/ppermute | solution.py:15
  532.7 11.5 %collective-permute-start.25 = (f32[4,128,128]{2,1,0:T(8,128)}, f32[4,128,128]{2,1,0:T(8,128)}, u32[]{:S(2)}, u32[]{:S(2)}) collective-permute-start(f32[4,128,128]{2,1,0:T(8,128)} %bitcast.298), channel_id=1, source_target_pairs={{1,0},{2,1},{3,2},{4,3},{5,4},{6,5},{7,6},{8,7},{9,8},{10,9},{11,1... | collective-permute-start | bytes 786440 | tf_op jit(solution)/shard_map/ppermute | solution.py:15
  534.8 11.6 %collective-permute-start.24 = (f32[4,128,128]{2,1,0:T(8,128)}, f32[4,128,128]{2,1,0:T(8,128)}, u32[]{:S(2)}, u32[]{:S(2)}) collective-permute-start(f32[4,128,128]{2,1,0:T(8,128)} %bitcast.296), channel_id=1, source_target_pairs={{0,1},{1,2},{2,3},{3,4},{4,5},{5,6},{6,7},{7,8},{8,9},{9,10},{10,1... | collective-permute-start | bytes 786440 | tf_op jit(solution)/shard_map/ppermute | solution.py:15
  631.3 99.3 %copy-start.1 = (f32[2048,128]{0,1:T(8,128)S(1)}, f32[2048,128]{0,1:T(8,128)}, u32[]{:S(2)}) copy-start(f32[2048,128]{0,1:T(8,128)} %copy-done) | copy-start | bytes 3145732
  631.3 99.3 %copy-start.7 = (f32[128]{0:T(128)S(1)}, f32[128]{0:T(128)}, u32[]{:S(2)}) copy-start(f32[128]{0:T(128)} %div.19) | copy-start | bytes 1540
  723.2 19.1 %collective-permute-start.31 = (f32[4,128,128]{2,1,0:T(8,128)}, f32[4,128,128]{2,1,0:T(8,128)}, u32[]{:S(2)}, u32[]{:S(2)}) collective-permute-start(f32[4,128,128]{2,1,0:T(8,128)} %bitcast.293), channel_id=1, source_target_pairs={{16,0},{32,16},{48,32},{64,48},{80,64},{96,80},{112,96},{128,112},... | collective-permute-start | bytes 786440 | tf_op jit(solution)/shard_map/ppermute | solution.py:15
  727.6 16.3 %collective-permute-start.30 = (f32[4,128,128]{2,1,0:T(8,128)}, f32[4,128,128]{2,1,0:T(8,128)}, u32[]{:S(2)}, u32[]{:S(2)}) collective-permute-start(f32[4,128,128]{2,1,0:T(8,128)} %bitcast.288), channel_id=1, source_target_pairs={{0,16},{16,32},{32,48},{48,64},{64,80},{80,96},{96,112},{112,128},... | collective-permute-start | bytes 786440 | tf_op jit(solution)/shard_map/ppermute | solution.py:15
  736.8 9.7 %collective-permute-start.29 = (f32[4,128,128]{2,1,0:T(8,128)S(1)}, f32[4,128,128]{2,1,0:T(8,128)S(1)}, u32[]{:S(2)}, u32[]{:S(2)}) collective-permute-start(f32[4,128,128]{2,1,0:T(8,128)S(1)} %bitcast.294), channel_id=1, source_target_pairs={{1,0},{2,1},{3,2},{4,3},{5,4},{6,5},{7,6},{8,7},{9,8},{10,9},{11,1... | collective-permute-start | bytes 786440 | tf_op jit(solution)/shard_map/ppermute | solution.py:15
  738.2 9.2 %collective-permute-start.28 = (f32[4,128,128]{2,1,0:T(8,128)S(1)}, f32[4,128,128]{2,1,0:T(8,128)S(1)}, u32[]{:S(2)}, u32[]{:S(2)}) collective-permute-start(f32[4,128,128]{2,1,0:T(8,128)S(1)} %bitcast.290), channel_id=1, source_target_pairs={{0,1},{1,2},{2,3},{3,4},{4,5},{5,6},{6,7},{7,8},{8,9},{9,10},{10,1... | collective-permute-start | bytes 786440 | tf_op jit(solution)/shard_map/ppermute | solution.py:15
where the time goes:
time: 820 us; the launch traced here: 808 us
  blocking collectives  491 us (60%)
  local copies, waits for them, and re-layouts  130 us (16%)
  starting transfers between devices  89.1 us (11%)
  other arithmetic  54.2 us (7%)
  matrix products  33.3 us (4%)
  waiting for transfers between devices  8.26 us (1%)
    psum x2, blocking collectives, project(): lax.psum(jnp.sum(weights * projected * projected, axis=0), ('cluster', 's...  147 us
    psum x3, blocking collectives, project(): cluster_terms = lax.psum(local_terms, 'sub')  91.1 us
    ppermute x32, starting transfers between devices, passed_along(): lax.ppermute(value, axis, [(source, source + steps) for source in range(l...  89.1 us
    psum x1, blocking collectives, per_device(): curvature = lax.psum(curvature_terms, ('cluster', 'sub'))  73.7 us
    all_gather x3, blocking collectives, project(): gathered = lax.all_gather(cluster_terms, 'cluster', axis=0, tiled=True)  69.8 us
    psum x1, blocking collectives, per_device(): cluster_rows = lax.psum(row_terms, 'sub')  58.8 us
    unnamed x56, local copies, waits for them, and re-layouts  38.6 us
    gather x32, local copies, waits for them, and re-layouts, neighbour_parts(): jnp.take(arrived, peer_table[:, facing], axis=0)  37 us
  transfers between devices with their start and end apart: 32, of which 5 were waited for; matrix products, arithmetic and copies ran while one was open for 11% of the time, Pallas kernels for 0%

commit v1 on v0

v1 whole, which is shorter than its diff:
```python
import functools

import jax
import jax.numpy as jnp
from jax import lax
from jax.experimental import pallas as pl
from jax.experimental.pallas import tpu as pltpu
from jax.sharding import PartitionSpec as P

MESH = pl.DeviceIdType.MESH
HIGHEST = lax.Precision.HIGHEST
F32 = jnp.float32
BF16 = jnp.bfloat16
MODES = 6
PAD = 8


def split(value):
    high = value.astype(BF16)
    low = (value - high.astype(F32)).astype(BF16)
    return high, low


def elimination_levels(count):
    levels, step = [], 1
    while step < count:
        levels.append(list(range(step, count, 2 * step)))
        step *= 2
    return levels + [[0]]


def coarse_inverse(tiles):
    count = len(tiles)
    rows = lax.broadcasted_iota(jnp.int32, (PAD, 128), 0)
    lanes = lax.broadcasted_iota(jnp.int32, (PAD, 128), 1)
    left = list(tiles)
    right = [
        jnp.where((lanes == rows + PAD * t) & (rows < MODES), 1.0, 0.0).astype(F32)
        for t in range(count)
    ]
    pattern = [[abs(t - u) <= 1 for u in range(count)] for t in range(count)]
    scale = [jnp.ones((PAD, 128), F32) for _ in range(count)]
    for level in elimination_levels(count):
        touched = {p: [t for t in range(count) if pattern[t][p]] for p in level}
        for mode in range(MODES):
            updates = []
            for p in level:
                column = PAD * p + mode
                factors = {
                    t: jnp.broadcast_to(left[t][:, column : column + 1], (PAD, 128))
                    for t in touched[p]
                }
                inverse = 1.0 / factors[p][mode : mode + 1, :]
                row_left = left[p][mode : mode + 1, :] * inverse
                row_right = right[p][mode : mode + 1, :] * inverse
                factors[p] = jnp.where(rows == mode, 0.0, factors[p])
                scale[p] = jnp.where(rows == mode, inverse, scale[p])
                updates.append((factors, row_left, row_right))
            for factors, row_left, row_right in updates:
                for t, factor in factors.items():
                    left[t] = left[t] - factor * row_left
                    right[t] = right[t] - factor * row_right
        for p in level:
            for t in touched[p]:
                for u in range(count):
                    pattern[t][u] = pattern[t][u] or pattern[p][u]
    return [r * k for r, k in zip(right, scale)]


def kernel(
    C,
    S,
    peer,
    sign,
    dual_hbm,
    load_hbm,
    modes_hbm,
    cload_hbm,
    out_hbm,
    amp_out,
    dual,
    load,
    modes,
    cload,
    lam,
    res,
    z0,
    z1,
    im0,
    im1,
    im2,
    halo00,
    halo01,
    halo02,
    halo03,
    halo10,
    halo11,
    halo12,
    halo13,
    rhs,
    gt,
    t3,
    cinv,
    ka,
    kb,
    ra,
    rb,
    lsem,
    osem,
    hsend,
    hrecv,
    asend,
    arecv,
    bsend,
    brecv,
):
    c = lax.axis_index("cluster")
    s = lax.axis_index("sub")
    has = [s > 0, s < S - 1, c > 0, c < C - 1]
    halo = [[halo00, halo01, halo02, halo03], [halo10, halo11, halo12, halo13]]

    cp_modes = pltpu.make_async_copy(modes_hbm, modes, lsem.at[0])
    cp_cload = pltpu.make_async_copy(cload_hbm, cload, lsem.at[1])
    cp_dual = pltpu.make_async_copy(dual_hbm, dual, lsem.at[2])
    cp_load = pltpu.make_async_copy(load_hbm, load, lsem.at[3])
    cp_modes.start()
    cp_cload.start()
    cp_dual.start()
    cp_load.start()

    barrier = pltpu.get_barrier_semaphore()

    def greet_sub(i, carry):
        pl.semaphore_signal(
            barrier, inc=1, device_id=(c, lax.rem(s + i, S)), device_id_type=MESH
        )
        return carry

    def greet_cluster(i, carry):
        pl.semaphore_signal(
            barrier, inc=1, device_id=(lax.rem(c + i, C), s), device_id_type=MESH
        )
        return carry

    lax.fori_loop(1, S, greet_sub, 0)
    lax.fori_loop(1, C, greet_cluster, 0)

    def send_sub(buf, k):
        def body(i, carry):
            pltpu.make_async_remote_copy(
                src_ref=buf.at[s],
                dst_ref=buf.at[s],
                send_sem=asend.at[k],
                recv_sem=arecv.at[k],
                device_id=(c, lax.rem(s + i, S)),
                device_id_type=MESH,
            ).start()
            return carry

        lax.fori_loop(1, S, body, 0)

    def send_cluster(buf, k):
        def body(i, carry):
            pltpu.make_async_remote_copy(
                src_ref=buf.at[c],
                dst_ref=buf.at[c],
                send_sem=bsend.at[k],
                recv_sem=brecv.at[k],
                device_id=(lax.rem(c + i, C), s),
                device_id_type=MESH,
            ).start()
            return carry

        lax.fori_loop(1, C, body, 0)

    def wait_bytes(buf, count, sem):
        part = buf.at[pl.ds(0, count - 1)]
        pltpu.make_async_copy(part, part, sem).wait()

    def sum_sub(buf):
        total = buf[0]
        for i in range(1, S):
            total = total + buf[i]
        return total

    def halo_copy(src, x, f):
        device = [(c, s - 1), (c, s + 1), (c - 1, s), (c + 1, s)][f]
        return pltpu.make_async_remote_copy(
            src_ref=src.at[f],
            dst_ref=halo[x][f ^ 1],
            send_sem=hsend.at[x, f],
            recv_sem=hrecv.at[x, f ^ 1],
            device_id=device,
            device_id_type=MESH,
        )

    def halo_arrived(src, x, f):
        pltpu.make_async_copy(halo[x][f], halo[x][f], hrecv.at[x, f]).wait()

    for f in range(4):

        @pl.when(jnp.logical_not(has[f]))
        def _():
            for x in range(2):
                halo[x][f][...] = jnp.zeros((4, 128, 128), F32)

    cp_modes.wait()
    cp_cload.wait()
    size = modes.shape[1]
    rows = jnp.concatenate([modes[...], jnp.zeros((PAD - MODES, size), F32)], axis=0)
    face = (lax.broadcasted_iota(jnp.int32, (PAD, size), 1) // 128) % 4
    at_rim0 = jnp.where(s > 0, 0.0, 1.0)
    at_rim1 = jnp.where(s < S - 1, 0.0, 1.0)
    low_on = jnp.where(c > 0, 1.0, 0.0)
    high_on = jnp.where(c < C - 1, 1.0, 0.0)
    rows2 = jnp.where(face == 2, rows, 0.0)
    rows3 = jnp.where(face == 3, rows, 0.0)
    own = jnp.where(face >= 2, rows, jnp.where(face == 0, rows * at_rim0, rows * at_rim1))
    span = jnp.concatenate([-low_on * rows2, own, -high_on * rows3], axis=0)

    coarse_row = lax.dot_general(
        rows, span, (((1,), (1,)), ((), ())), precision=HIGHEST, preferred_element_type=F32
    )
    coarse_row = jnp.concatenate([coarse_row, jnp.zeros((PAD, 128 - 3 * PAD), F32)], axis=1)
    shift = lax.rem(PAD * c + 128 - PAD, 128)
    ka[s] = pltpu.roll(coarse_row, shift, 1)

    pl.semaphore_wait(barrier, S - 1 + C - 1)
    send_sub(ka, 0)

    by_face = [
        jnp.concatenate(
            [part[:, 128 * (4 * k + f) : 128 * (4 * k + f + 1)] for f in range(4) for k in range(4)],
            axis=1,
        )
        for part in (own, rows2, rows3)
    ]
    t3_high, t3_low = split(jnp.concatenate(by_face, axis=0))
    t3[...] = jnp.concatenate([t3_high, t3_low], axis=0)
    span_high = span.astype(BF16).astype(F32)
    wide = jnp.concatenate(
        [span_high, span - span_high, span_high, jnp.zeros((128 - 9 * PAD, size), F32)], axis=0
    )
    for b in range(16):
        gt[b // 4, b % 4] = wide[:, 128 * b : 128 * (b + 1)].T.astype(BF16)

    wait_bytes(ka, S, arecv.at[0])
    kb[c, 0:PAD] = sum_sub(ka)
    kb[c, PAD : 2 * PAD] = jnp.concatenate(
        [cload[...], jnp.zeros((PAD - MODES, 128), F32)], axis=0
    )
    send_cluster(kb, 0)
    wait_bytes(kb, C, brecv.at[0])

    inverse = coarse_inverse([kb[t, 0:PAD] for t in range(C)])
    zero_tile = jnp.zeros((PAD, 128), F32)
    cinv[0:PAD] = zero_tile
    for t in range(C):
        cinv[PAD * (t + 1) : PAD * (t + 2)] = inverse[t]
    cinv[PAD * (C + 1) : PAD * (C + 2)] = zero_tile

    def stacked(parts):
        value = jnp.concatenate(parts, axis=0)
        if value.shape[0] < 128:
            value = jnp.concatenate([value, jnp.zeros((128 - value.shape[0], 128), F32)], axis=0)
        return value

    def near_solve(right):
        return jnp.dot(cinv[pl.ds(PAD * c, 3 * PAD), :], right, precision=HIGHEST)

    def packed(amplitudes):
        high = amplitudes.astype(BF16).astype(F32)
        return jnp.concatenate(
            [high, high, amplitudes - high, jnp.zeros((128 - 9 * PAD, 128), F32)], axis=0
        ).astype(BF16)

    def spread(weights, k, f):
        return jnp.dot(gt[k, f], weights, preferred_element_type=F32)

    def restricted(field):
        value = field[...].reshape(size, 128)
        high, low = split(value)
        pair = jnp.dot(
            t3[...], jnp.concatenate([high, low], axis=1), preferred_element_type=F32
        )
        half = 3 * PAD
        return pair[:half, :128] + (pair[half:, :128] + pair[:half, 128:]) + pair[half:, 128:]

    def joined(buf):
        parts = []
        for t in range(C):
            part = buf[t, 0:PAD]
            if t > 0:
                part = part - buf[t - 1, 2 * PAD : 3 * PAD]
            if t < C - 1:
                part = part - buf[t + 1, PAD : 2 * PAD]
            parts.append(part)
        return stacked(parts)

    def scalar_total(buf, row):
        total = buf[0, row : row + 1]
        for t in range(1, C):
            total = total + buf[t, row : row + 1]
        return total

    row_ids = lax.broadcasted_iota(jnp.int32, (3 * PAD, 128), 0)

    def reduce_start(k, terms, scalars):
        for row, value in scalars:
            terms = jnp.where(row_ids == row, value, terms)
        ra[k, s] = terms
        send_sub(ra.at[k], k + 1)

    def reduce_end(k):
        wait_bytes(ra.at[k], S, arecv.at[k + 1])
        rb[k, c] = sum_sub(ra.at[k])
        send_cluster(rb.at[k], k + 1)
        wait_bytes(rb.at[k], C, brecv.at[k + 1])

    half_on = [jnp.where(has[f], 0.5, 1.0) for f in range(4)]

    def column_sum(parts):
        return jnp.sum(parts, axis=0, keepdims=True)

    start = near_solve(stacked([kb[t, PAD : 2 * PAD] for t in range(C)]))
    weights = packed(start)
    for b in range(16):
        k, f = b // 4, b % 4
        value = spread(weights, k, f)
        lam[k, f] = value
        rhs[k, f, :, 0:128] = value.astype(BF16)

    cp_dual.wait()
    cp_load.wait()
    for f in range(4):
        part = jnp.dot(
            dual[:, f].reshape(size // 4, size),
            rhs[:, :, :, 0:128].reshape(size, 128),
            preferred_element_type=F32,
        )
        im0[f] = load[:, f] - part.reshape(4, 128, 128)

        @pl.when(has[f])
        def _():
            halo_copy(im0, 0, f).start()

    reduce_start(0, restricted(im0), [])
    reduce_end(0)
    coarse_now = joined(rb.at[0])
    weights = packed(near_solve(coarse_now))
    for f in range(4):

        @pl.when(has[f])
        def _():
            halo_arrived(im0, 0, f)

    norm = jnp.zeros((PAD, 128), F32)
    for b in range(16):
        k, f = b // 4, b % 4
        value = im0[f, k] - halo[0][f][peer[0, 0, b]]
        res[k, f] = value
        value = value - spread(weights, k, f)
        z0[k, f] = value
        rhs[k, f, :, 0:128] = value.astype(BF16)
        norm = norm + half_on[f] * jnp.sum((value * value).reshape(16, PAD, 128), axis=0)
    norm = column_sum(norm)

    curvature = jnp.zeros((PAD, 128), F32)
    for f in range(4):
        part = jnp.dot(
            dual[:, f].reshape(size // 4, size),
            rhs[:, :, :, 0:128].reshape(size, 128),
            preferred_element_type=F32,
        ).reshape(4, 128, 128)
        im1[f] = part
        signed = rhs[:, f, :, 0:128].astype(F32)
        curvature = curvature + jnp.sum((signed * part).reshape(64, PAD, 128), axis=0)

        @pl.when(has[f])
        def _():
            halo_copy(im1, 1, f).start()

    reduce_start(1, restricted(im1), [(6, norm), (7, column_sum(curvature))])
    reduce_end(1)
    norm_now = scalar_total(rb.at[1], 6)
    curvature_now = scalar_total(rb.at[1], 7)
    length = norm_now / curvature_now
    coarse_image = joined(rb.at[1])
    coarse_now = coarse_now - length * coarse_image
    weights = packed(near_solve(coarse_now))
    for f in range(4):

        @pl.when(has[f])
        def _():
            halo_arrived(im1, 1, f)

    norm = jnp.zeros((PAD, 128), F32)
    cross = jnp.zeros((PAD, 128), F32)
    for b in range(16):
        k, f = b // 4, b % 4
        value = res[k, f] - length * (im1[f, k] - halo[1][f][peer[0, 0, b]])
        value = value - spread(weights, k, f)
        z1[k, f] = value
        high, low = split(value)
        rhs[k, f, :, 0:128] = high
        rhs[k, f, :, 128:256] = low
        lam[k, f] = lam[k, f] + length * z0[k, f]
        norm = norm + half_on[f] * jnp.sum((value * value).reshape(16, PAD, 128), axis=0)
        cross = cross + jnp.sum((value * im1[f, k]).reshape(16, PAD, 128), axis=0)

    curvature = jnp.zeros((PAD, 128), F32)
    for f in range(4):
        pair = jnp.dot(
            dual[:, f].reshape(size // 4, size),
            rhs[...].reshape(size, 256),
            preferred_element_type=F32,
        )
        part = (pair[:, :128] + pair[:, 128:]).reshape(4, 128, 128)
        im2[f] = part
        curvature = curvature + jnp.sum((z1[:, f] * part).reshape(64, PAD, 128), axis=0)

    reduce_start(
        2,
        restricted(im2),
        [(6, column_sum(norm)), (7, column_sum(curvature)), (14, column_sum(cross))],
    )
    reduce_end(2)
    norm_next = scalar_total(rb.at[2], 6)
    ratio = norm_next / norm_now
    curvature_next = (
        scalar_total(rb.at[2], 7)
        + 2.0 * ratio * scalar_total(rb.at[2], 14)
        + ratio * ratio * curvature_now
    )
    length = norm_next / curvature_next
    coarse_now = coarse_now - length * (joined(rb.at[2]) + ratio * coarse_image)
    last = jnp.dot(cinv[pl.ds(PAD * (c + 1), PAD), :], coarse_now, precision=HIGHEST)
    amp_out[0] = last[:MODES]

    copies = []
    for b in range(16):
        k, f = b // 4, b % 4
        turned = sign[0, 0, b].astype(F32)
        value = lam[k, f] + length * (z1[k, f] + ratio * z0[k, f])
        lam[k, f] = turned * value
        copy = pltpu.make_async_copy(lam.at[k, f], out_hbm.at[k, f], osem.at[b])
        copy.start()
        copies.append(copy)

    for k in range(4):
        wait_bytes(ka if k == 0 else ra.at[k - 1], S, asend.at[k])
        wait_bytes(kb if k == 0 else rb.at[k - 1], C, bsend.at[k])
    for f in range(4):

        @pl.when(has[f])
        def _():
            halo_copy(im0, 0, f).wait_send()
            halo_copy(im1, 1, f).wait_send()

    for copy in copies:
        copy.wait()


def per_device(C, S, dual_ops, local_load, rigid_modes, coarse_load, gluing_peer, gluing_sign):
    size = dual_ops.shape[-1]
    block = size // 16
    loads = local_load.shape[-1]
    any_space = pl.BlockSpec(memory_space=pl.ANY)
    smem = pl.BlockSpec(memory_space=pltpu.SMEM)
    field = pltpu.VMEM((4, 4, block, loads), F32)
    multipliers, amplitudes = pl.pallas_call(
        functools.partial(kernel, C, S),
        out_shape=(
            jax.ShapeDtypeStruct((4, 4, block, loads), F32),
            jax.ShapeDtypeStruct((1, MODES, loads), F32),
        ),
        in_specs=[smem, smem] + [any_space] * 4,
        out_specs=(any_space, pl.BlockSpec(memory_space=pltpu.VMEM)),
        scratch_shapes=[
            pltpu.VMEM((4, 4, block, size), BF16),
            field,
            pltpu.VMEM((MODES, size), F32),
            pltpu.VMEM((MODES, loads), F32),
            field,
            field,
            field,
            field,
            field,
            field,
            field,
        ]
        + [pltpu.VMEM((4, block, loads), F32)] * 8
        + [
            pltpu.VMEM((4, 4, block, 2 * loads), BF16),
            pltpu.VMEM((4, 4, block, 128), BF16),
            pltpu.VMEM((6 * PAD, size), BF16),
            pltpu.VMEM((PAD * (C + 2), 128), F32),
            pltpu.VMEM((S, PAD, 128), F32),
            pltpu.VMEM((C, 2 * PAD, 128), F32),
            pltpu.VMEM((3, S, 3 * PAD, 128), F32),
            pltpu.VMEM((3, C, 3 * PAD, 128), F32),
            pltpu.SemaphoreType.DMA((4,)),
            pltpu.SemaphoreType.DMA((16,)),
            pltpu.SemaphoreType.DMA((2, 4)),
            pltpu.SemaphoreType.DMA((2, 4)),
            pltpu.SemaphoreType.DMA((4,)),
            pltpu.SemaphoreType.DMA((4,)),
            pltpu.SemaphoreType.DMA((4,)),
            pltpu.SemaphoreType.DMA((4,)),
        ],
        compiler_params=pltpu.CompilerParams(
            collective_id=0, has_side_effects=True, vmem_limit_bytes=48 * 1024 * 1024
        ),
    )(
        gluing_peer,
        gluing_sign,
        dual_ops.reshape(4, 4, block, size),
        local_load.reshape(4, 4, block, loads),
        rigid_modes[0, 0],
        coarse_load[0],
    )
    return multipliers.reshape(1, 1, size, loads), amplitudes


def solution(mesh):
    return jax.shard_map(
        functools.partial(per_device, mesh.shape["cluster"], mesh.shape["sub"]),
        mesh=mesh,
        in_specs=(
            P("cluster", "sub", None, None),
            P("cluster", "sub", None, None),
            P("cluster", "sub", None, None),
            P("cluster", None, None),
            P("cluster", "sub", None),
            P("cluster", "sub", None),
        ),
        out_specs=(P("cluster", "sub", None, None), P("cluster", None, None)),
        check_vma=False,
    )
```

time: 820 us -> 90.4 us (0.11); the launches traced: 808 us -> 90.1 us
  blocking collectives: 491 us -> 0 us
  local copies, waits for them, and re-layouts: 130 us -> 5.58 us
  starting transfers between devices: 89.1 us -> 0 us
  Pallas kernels: 0 us -> 83.9 us
  other arithmetic: 54.2 us -> 0 us
  matrix products: 33.3 us -> 0 us
  waiting for transfers between devices: 8.26 us -> 0 us
    psum x7 -> x0, blocking collectives: 371 us -> none  [the longest x2 147 us: project(): lax.psum(jnp.sum(weights * projected * projected, axis=0), ('cluster', 's...]
    all_gather x5 -> x0, blocking collectives: 120 us -> none  [the longest x3 69.8 us: project(): gathered = lax.all_gather(cluster_terms, 'cluster', axis=0, tiled=True)]
    ppermute x32 -> x0, starting transfers between devices: 89.1 us -> none  [passed_along(): lax.ppermute(value, axis, [(source, source + steps) for source in range(l...]
    pallas_call x0 -> x1, Pallas kernels: none -> 83.9 us  [per_device(): pl.pallas_call(functools.partial(kernel, C, S), out_shape=(jax.ShapeDtype...]
    another operation x42 -> x0, other arithmetic: 37.7 us -> none  [the longest x36 19.4 us: place(): return jnp.stack(pieces, axis=1).reshape(dual_size, breadth)]
    gather x32 -> x0, local copies, waits for them, and re-layouts: 37 us -> none  [neighbour_parts(): jnp.take(arrived, peer_table[:, facing], axis=0)]
    unnamed x56 -> x10, local copies, waits for them, and re-layouts: 38.6 us -> 5.58 us
    dot_general x11 -> x0, matrix products: 31.5 us -> none  [the longest x3 21.6 us: dual_images(): images = jnp.dot(operator, signed, preferred_element_type=jnp.float32)]
  transfers between devices with their start and end apart: 32 -> 0, of which waited for: 5 -> 0; matrix products, arithmetic and copies ran while one was open for 11% -> 0% of each run, Pallas kernels for 0% -> 0%
where the time goes in v1:
time: 90.4 us; the launch traced here: 90.1 us
  Pallas kernels  83.9 us (93%)
  local copies, waits for them, and re-layouts  5.58 us (6%)
    pallas_call x1, Pallas kernels, per_device(): pl.pallas_call(functools.partial(kernel, C, S), out_shape=(jax.ShapeDtype...  83.9 us
    unnamed x10, local copies, waits for them, and re-layouts  5.58 us

profile of v1, /device:TPU:1, one launch (start us, length us, event | category | flops | bytes accessed | tf_op | source)
XLA Modules:
  0.0 90.1 jit_solution(16322418815630142407)
XLA Ops:
  0.6 0.7 copy.14
  1.3 0.8 copy.13
  2.1 0.0 copy-start
  2.1 1.2 %copy-done = f32[1,1,2048,128]{3,2,1,0:T(8,128)S(1)} copy-done((f32[1,1,2048,128]{3,2,1,0:T(8,128)S(1)}, f32[1,1,2048,128]{3,2,1,0:T(8,128)}, u32[]{:S(2)}) %copy-start) | copy-done | bytes 1048600
  3.4 0.0 copy-start.1
  3.4 0.7 copy-done.1
  4.0 0.0 copy-start.2
  4.0 0.7 copy-done.2
  4.7 83.9 %shard_map.77 = (f32[4,4,128,128]{3,2,1,0:T(8,128)S(1)}, f32[1,6,128]{2,1,0:T(8,128)S(1)}) custom-call(s32[1,1,16]{2,1,0:T(1,128)S(1)} %copy-done.1, s32[1,1,16]{2,1,0:T(1,128)S(1)} %copy-done.2, bf16[4,4,128,2048]{3,2,1,0:T(8,128)(2,1)} %bitcast.13, f32[4,4,128,128]{3,2,1,0:T(8,128)S(1)} %bitcast.9, f32[6,2048]{1,0:T(8,128)S(1)} %bitcast.11, ...), custom_call_target="tpu_custom_call" | custom-call | tf_op jit(solution)/shard_map/pallas_call | solution.py:471
  88.6 0.6 copy.8
  89.2 1.0 %copy.16 = f32[1,1,2048,128]{3,2,1,0:T(8,128)} copy(f32[1,1,2048,128]{3,2,1,0:T(8,128)S(1)} %bitcast.10) | data formatting | bytes 2097152
Async XLA Ops:
  2.1 1.2 %copy-start = (f32[1,1,2048,128]{3,2,1,0:T(8,128)S(1)}, f32[1,1,2048,128]{3,2,1,0:T(8,128)}, u32[]{:S(2)}) copy-start(f32[1,1,2048,128]{3,2,1,0:T(8,128)} %param.7) | copy-start | bytes 3145732
  3.4 0.7 copy-start.1
  4.0 0.7 copy-start.2

commit v2 on v0

v2 whole, which is shorter than its diff:
```python
import functools
import types

import jax
import jax.numpy as jnp
from jax import lax
from jax.experimental import pallas as pl
from jax.experimental.pallas import tpu as pltpu
from jax.sharding import PartitionSpec as P

MESH = pl.DeviceIdType.MESH
HIGHEST = lax.Precision.HIGHEST
F32 = jnp.float32
BF16 = jnp.bfloat16
MODES = 6
PAD = 8


def split(value):
    high = value.astype(BF16)
    low = (value - high.astype(F32)).astype(BF16)
    return high, low


def elimination_levels(count):
    levels, step = [], 1
    while step < count:
        levels.append(list(range(step, count, 2 * step)))
        step *= 2
    return levels + [[0]]


def coarse_inverse(tiles):
    count = len(tiles)
    rows = lax.broadcasted_iota(jnp.int32, (PAD, 128), 0)
    lanes = lax.broadcasted_iota(jnp.int32, (PAD, 128), 1)
    left = list(tiles)
    right = [
        jnp.where((lanes == rows + PAD * t) & (rows < MODES), 1.0, 0.0).astype(F32)
        for t in range(count)
    ]
    pattern = [[abs(t - u) <= 1 for u in range(count)] for t in range(count)]
    scale = [jnp.ones((PAD, 128), F32) for _ in range(count)]
    for level in elimination_levels(count):
        touched = {p: [t for t in range(count) if pattern[t][p]] for p in level}
        for mode in range(MODES):
            updates = []
            for p in level:
                column = PAD * p + mode
                factors = {
                    t: jnp.broadcast_to(left[t][:, column : column + 1], (PAD, 128))
                    for t in touched[p]
                }
                inverse = 1.0 / factors[p][mode : mode + 1, :]
                row_left = left[p][mode : mode + 1, :] * inverse
                row_right = right[p][mode : mode + 1, :] * inverse
                factors[p] = jnp.where(rows == mode, 0.0, factors[p])
                scale[p] = jnp.where(rows == mode, inverse, scale[p])
                updates.append((factors, row_left, row_right))
            for factors, row_left, row_right in updates:
                for t, factor in factors.items():
                    left[t] = left[t] - factor * row_left
                    right[t] = right[t] - factor * row_right
        for p in level:
            for t in touched[p]:
                for u in range(count):
                    pattern[t][u] = pattern[t][u] or pattern[p][u]
    return [r * k for r, k in zip(right, scale)]


NAMES = (
    "peer_hbm",
    "dual_hbm",
    "load_hbm",
    "modes_hbm",
    "cload_hbm",
    "lam_hbm",
    "z0_hbm",
    "w_hbm",
    "last_out",
    "peer",
    "dual",
    "load",
    "modes",
    "cload",
    "lam",
    "z0",
    "y",
    "im0",
    "h00",
    "h01",
    "h02",
    "h03",
    "h10",
    "h11",
    "h12",
    "h13",
    "a0",
    "a1",
    "a2",
    "a3",
    "r0",
    "r1",
    "r2",
    "r3",
    "rhs",
    "basis",
    "t3",
    "d3",
    "cinv",
    "coef",
    "msg",
    "ka",
    "kb",
    "eb",
    "ra0",
    "rb0",
    "ra2",
    "rb2",
    "ra3",
    "ub3",
    "rb3",
    "sa",
    "sb",
    "lsem",
    "osem",
    "hsend",
    "hrecv",
    "gsend",
    "grecv",
    "asend",
    "arecv",
    "bsend",
    "brecv",
    "ksend",
    "krecv",
    "esend",
    "erecv",
)


def kernel(C, S, *refs):
    r = types.SimpleNamespace(**dict(zip(NAMES, refs)))
    c = lax.axis_index("cluster")
    s = lax.axis_index("sub")
    Z = C // 2
    z, core = c // 2, lax.rem(c, 2)
    has = [s > 0, s < S - 1, c > 0, c < C - 1]
    towards = [(c, s - 1), (c, s + 1), (c - 1, s), (c + 1, s)]
    halo = [[r.h00, r.h01, r.h02, r.h03], [r.h10, r.h11, r.h12, r.h13]]
    near_modes = [r.a0, r.a1, r.a2, r.a3]
    turned_modes = [r.r0, r.r1, r.r2, r.r3]
    size = r.dual.shape[3]

    cp_modes = pltpu.make_async_copy(r.modes_hbm, r.modes, r.lsem.at[0])
    cp_cload = pltpu.make_async_copy(r.cload_hbm, r.cload, r.lsem.at[1])
    cp_dual = pltpu.make_async_copy(r.dual_hbm, r.dual, r.lsem.at[2])
    cp_load = [
        pltpu.make_async_copy(r.load_hbm.at[:, f], r.load.at[f], r.lsem.at[3 + f]) for f in range(4)
    ]
    cp_peer = pltpu.make_async_copy(r.peer_hbm, r.peer, r.lsem.at[7])
    cp_modes.start()
    cp_peer.start()
    cp_cload.start()
    for copy in cp_load:
        copy.start()
    cp_dual.start()

    barrier = pltpu.get_barrier_semaphore()

    def greet_sub(i, carry):
        pl.semaphore_signal(
            barrier, inc=1, device_id=(c, lax.rem(s + i, S)), device_id_type=MESH
        )
        return carry

    def greet_cluster(i, carry):
        pl.semaphore_signal(
            barrier, inc=1, device_id=(lax.rem(c + i, C), s), device_id_type=MESH
        )
        return carry

    lax.fori_loop(1, S, greet_sub, 0)
    lax.fori_loop(1, C, greet_cluster, 0)

    def send(src, dst, send_sem, recv_sem, device):
        pltpu.make_async_remote_copy(
            src_ref=src,
            dst_ref=dst,
            send_sem=send_sem,
            recv_sem=recv_sem,
            device_id=device,
            device_id_type=MESH,
        ).start()

    def wait_bytes(part, sem):
        pltpu.make_async_copy(part, part, sem).wait()

    def sub_start(buf, k):
        def body(i, carry):
            send(buf.at[s], buf.at[s], r.asend.at[k], r.arecv.at[k], (c, lax.rem(s + i, S)))
            return carry

        lax.fori_loop(1, S, body, 0)

    def sub_total(buf, k):
        wait_bytes(buf.at[pl.ds(0, S - 1)], r.arecv.at[k])
        total = buf[0]
        for i in range(1, S):
            total = total + buf[i]
        return total

    def chips_start(buf, k):
        def body(i, carry):
            there = lax.rem(z + i, Z) * 2 + core
            send(buf.at[core, z], buf.at[core, z], r.bsend.at[k], r.brecv.at[k], (there, s))
            return carry

        lax.fori_loop(1, Z, body, 0)

    def cores_start(buf, k):
        wait_bytes(buf.at[0, pl.ds(0, Z - 1)], r.brecv.at[k])
        send(buf.at[core], buf.at[core], r.ksend.at[k], r.krecv.at[k], (2 * z + 1 - core, s))

    def cores_end(buf, k):
        wait_bytes(buf.at[0], r.krecv.at[k])

    def cluster_start(src, buf, k):
        def body(i, carry):
            there = lax.rem(c + i, C)
            send(src(there), buf.at[c], r.bsend.at[k], r.brecv.at[k], (there, s))
            return carry

        lax.fori_loop(1, C, body, 0)

    def cluster_total(buf, k):
        wait_bytes(buf.at[pl.ds(0, C - 1)], r.brecv.at[k])
        total = buf[0]
        for t in range(1, C):
            total = total + buf[t]
        return total

    def at_cluster(buf, t):
        return buf.at[t % 2, t // 2]

    def halo_copy(src, x, f):
        return pltpu.make_async_remote_copy(
            src_ref=src.at[f],
            dst_ref=halo[x][f ^ 1],
            send_sem=r.hsend.at[x, f],
            recv_sem=r.hrecv.at[x, f ^ 1],
            device_id=towards[f],
            device_id_type=MESH,
        )

    def modes_copy(f):
        return pltpu.make_async_remote_copy(
            src_ref=r.msg.at[f],
            dst_ref=near_modes[f ^ 1],
            send_sem=r.gsend.at[f],
            recv_sem=r.grecv.at[f ^ 1],
            device_id=towards[f],
            device_id_type=MESH,
        )

    for f in range(4):

        @pl.when(jnp.logical_not(has[f]))
        def _():
            for x in range(2):
                halo[x][f][...] = jnp.zeros((4, 128, 128), F32)
            near_modes[f][...] = jnp.zeros((128, 128), F32)

    r.coef[...] = jnp.zeros(r.coef.shape, F32)

    cp_modes.wait()
    cp_peer.wait()
    rows = jnp.concatenate([r.modes[:, b] for b in range(16)], axis=1)
    rows = jnp.concatenate([rows, jnp.zeros((PAD - MODES, size), F32)], axis=0)
    face = (lax.broadcasted_iota(jnp.int32, (PAD, size), 1) // 128) % 4
    at_rim0 = jnp.where(s > 0, 0.0, 1.0)
    at_rim1 = jnp.where(s < S - 1, 0.0, 1.0)
    low_on = jnp.where(c > 0, 1.0, 0.0)
    high_on = jnp.where(c < C - 1, 1.0, 0.0)
    rows2 = jnp.where(face == 2, rows, 0.0)
    rows3 = jnp.where(face == 3, rows, 0.0)
    own = jnp.where(face >= 2, rows, jnp.where(face == 0, rows * at_rim0, rows * at_rim1))
    span = jnp.concatenate([-low_on * rows2, own, -high_on * rows3], axis=0)

    coarse_row = lax.dot_general(
        rows, span, (((1,), (1,)), ((), ())), precision=HIGHEST, preferred_element_type=F32
    )
    coarse_row = jnp.concatenate([coarse_row, jnp.zeros((PAD, 128 - 3 * PAD), F32)], axis=1)
    r.ka[s] = pltpu.roll(coarse_row, lax.rem(PAD * c + 128 - PAD, 128), 1)

    cp_cload.wait()
    r.eb[c] = jnp.concatenate(
        [r.cload[:, 0], jnp.zeros((PAD - MODES, 128), F32)], axis=0
    )

    by_face = [
        jnp.concatenate(
            [part[:, 128 * (4 * k + f) : 128 * (4 * k + f + 1)] for f in range(4) for k in range(4)],
            axis=1,
        )
        for part in (own, rows2, rows3)
    ]
    t3_high, t3_low = split(jnp.concatenate(by_face, axis=0))
    r.t3[...] = jnp.concatenate([t3_high, t3_low], axis=0)
    span_high = span.astype(BF16).astype(F32)
    gap = jnp.zeros((PAD, size), F32)
    wide = jnp.concatenate(
        [span_high, gap, span - span_high, gap, span_high, gap, gap, gap, gap, gap], axis=0
    )
    for b in range(16):
        r.basis[b // 4, b % 4, :, 256:384] = wide[:, 128 * b : 128 * (b + 1)].T.astype(BF16)

    lanes = lax.broadcasted_iota(jnp.int32, (128, 128), 1)

    def tripled(value):
        high = value.astype(BF16).astype(F32)
        return (high + pltpu.roll(value - high, 32, 1) + pltpu.roll(high, 64, 1)).astype(BF16)

    cp_dual.wait()
    turned = []
    for f in range(4):
        part = jnp.dot(
            r.dual[:, f].reshape(size // 4, size),
            r.basis[:, :, :, 256:384].reshape(size, 128),
            preferred_element_type=F32,
        ).reshape(4, 128, 128)
        side = None
        for k in range(4):
            block = jnp.where(lanes < 3 * PAD, part[k] + pltpu.roll(part[k], 96, 1), 0.0)
            r.im0[f, k] = block
            turned.append(block.T[0 : 3 * PAD])
            r.basis[k, f, :, 0:128] = tripled(block)
            side = block if side is None else side + pltpu.roll(block, 32 * k, 1)
        r.msg[f] = side
    d3_high, d3_low = split(jnp.concatenate(turned, axis=1))
    r.d3[...] = jnp.concatenate([d3_high, d3_low], axis=0)

    def rows_times(left, high, low):
        pair = jnp.dot(
            left[...], jnp.concatenate([high, low], axis=1), preferred_element_type=F32
        )
        half = 3 * PAD
        return pair[:half, :128] + (pair[half:, :128] + pair[:half, 128:]) + pair[half:, 128:]

    def field_terms(left, field):
        return rows_times(left, *split(field[...].reshape(size, 128)))

    for copy in cp_load:
        copy.wait()
    mode_terms = field_terms(r.t3, r.im0)
    r.ra0[s, 0 : 3 * PAD] = field_terms(r.t3, r.load)
    r.ra0[s, 3 * PAD : 4 * PAD] = (
        mode_terms[0:PAD]
        + pltpu.roll(mode_terms[PAD : 2 * PAD], 32, 1)
        + pltpu.roll(mode_terms[2 * PAD : 3 * PAD], 64, 1)
    )

    pl.semaphore_wait(barrier, S - 1 + C - 1)
    sub_start(r.ka, 0)
    sub_start(r.ra0, 1)

    def send_e(i, carry):
        send(r.eb.at[c], r.eb.at[c], r.esend, r.erecv, (lax.rem(c + i, C), s))
        return carry

    lax.fori_loop(1, C, send_e, 0)

    for f in range(4):

        @pl.when(has[f])
        def _():
            halo_copy(r.load, 0, f).start()

    r.kb[c] = sub_total(r.ka, 0)
    cluster_start(lambda there: r.kb.at[c], r.kb, 0)
    r.rb0[core, z] = sub_total(r.ra0, 1)
    chips_start(r.rb0, 1)
    for f in range(4):

        @pl.when(has[f])
        def _():
            modes_copy(f).start()

    cores_start(r.rb0, 1)
    wait_bytes(r.kb.at[pl.ds(0, C - 1)], r.brecv.at[0])
    inverse = coarse_inverse([r.kb[t] for t in range(C)])
    zero_tile = jnp.zeros((PAD, 128), F32)
    r.cinv[0:PAD] = zero_tile
    for t in range(C):
        r.cinv[PAD * (t + 1) : PAD * (t + 2)] = inverse[t]
    r.cinv[PAD * (C + 1) : PAD * (C + 2)] = zero_tile

    def filled(value):
        if value.shape[0] < 128:
            value = jnp.concatenate([value, jnp.zeros((128 - value.shape[0], 128), F32)], axis=0)
        return value

    def solve(right):
        return jnp.dot(r.cinv[PAD : PAD * (C + 1), :], right, precision=HIGHEST)

    def keep(k, value):
        r.coef[k, 2 * PAD : PAD * (C + 2)] = value

    def near(k, offset):
        return r.coef[k, pl.ds(PAD * (c + 1 + offset), 3 * PAD), :]

    def packed(value):
        high = value.astype(BF16).astype(F32)
        empty = jnp.zeros((PAD, 128), F32)
        return jnp.concatenate(
            [high, empty, high, empty, value - high, empty, empty, empty, empty, empty], axis=0
        ).astype(BF16)

    wait_bytes(r.eb.at[pl.ds(0, C - 1)], r.erecv)
    start = solve(filled(jnp.concatenate([r.eb[t] for t in range(C)], axis=0)))
    keep(0, start)
    start = filled(start)

    for f in range(4):

        @pl.when(has[f])
        def _():
            wait_bytes(halo[0][f], r.hrecv.at[0, f])
            wait_bytes(near_modes[f], r.grecv.at[f])

    start_here = packed(near(0, 0))
    start_near = [start_here, start_here, packed(near(0, -1)), packed(near(0, 1))]
    for f in range(4):
        for j in range(4):
            group = r_f = near_modes[f][...]
            if j:
                group = pltpu.roll(r_f, 128 - 32 * j, 1)
            turned_modes[f][j] = jnp.where(lanes < 3 * PAD, group, 0.0)
        for k in range(4):
            r.basis[k, f, :, 128:256] = tripled(turned_modes[f][r.peer[0, 0, 4 * k + f]])
        image = jnp.dot(
            r.basis[:, f, :, 0:256].reshape(size // 4, 256),
            jnp.concatenate([start_here, -start_near[f]], axis=0),
            preferred_element_type=F32,
        ).reshape(4, 128, 128)
        spread_start = jnp.dot(
            r.basis[:, f, :, 256:384].reshape(size // 4, 128),
            start_here,
            preferred_element_type=F32,
        ).reshape(4, 128, 128)
        r.lam[f] = spread_start
        for k in range(4):
            r.z0[f, k] = r.load[f, k] - halo[0][f][r.peer[0, 0, 4 * k + f]] - image[k]

    out_lam = pltpu.make_async_copy(r.lam, r.lam_hbm, r.osem.at[0])
    out_lam.start()

    def joined(tile):
        parts = []
        for t in range(C):
            part = tile(t, 0)
            if t > 0:
                part = part - tile(t - 1, 2)
            if t < C - 1:
                part = part - tile(t + 1, 1)
            parts.append(part)
        return filled(jnp.concatenate(parts, axis=0))

    def term(buf):
        return lambda t, kind: at_cluster(buf, t)[PAD * kind : PAD * (kind + 1)]

    tile_lanes = lax.broadcasted_iota(jnp.int32, (PAD, 128), 1)

    def mode_term(t, kind):
        value = at_cluster(r.rb0, t)[3 * PAD : 4 * PAD]
        value = jnp.where((tile_lanes >= 32 * kind) & (tile_lanes < 32 * kind + 3 * PAD), value, 0.0)
        turn = (PAD * (t - 1) - 32 * kind) % 128
        return pltpu.roll(value, turn, 1) if turn else value

    cores_end(r.rb0, 1)
    gfg = joined(mode_term)
    coarse_now = joined(term(r.rb0)) - jnp.dot(gfg, start, precision=HIGHEST)
    first = solve(coarse_now)
    keep(1, first)
    weights = packed(near(1, 0))

    half_on = [jnp.where(has[f], 0.5, 1.0) for f in range(4)]

    def folded(value):
        return jnp.sum(value.reshape(-1, PAD, 128), axis=0)

    def column_sum(parts):
        return jnp.sum(parts, axis=0, keepdims=True)

    def spread(weights, f):
        return jnp.dot(
            r.basis[:, f, :, 256:384].reshape(size // 4, 128), weights, preferred_element_type=F32
        ).reshape(4, 128, 128)

    row_ids = lax.broadcasted_iota(jnp.int32, (3 * PAD, 128), 0)

    def with_rows(terms, scalars):
        for row, value in scalars:
            terms = jnp.where(row_ids == row, value, terms)
        return terms

    norm = jnp.zeros((PAD, 128), F32)
    for f in range(4):
        value = r.z0[f] - spread(weights, f)
        r.z0[f] = value
        r.rhs[:, f, :, 0:128] = value.astype(BF16)
        norm = norm + half_on[f] * folded(value * value)
    out_z0 = pltpu.make_async_copy(r.z0, r.z0_hbm, r.osem.at[1])
    out_z0.start()
    r.ra2[s] = with_rows(field_terms(r.d3, r.z0), [(6, column_sum(norm))])
    sub_start(r.ra2, 2)

    for f in range(4):
        r.im0[f] = jnp.dot(
            r.dual[:, f].reshape(size // 4, size),
            r.rhs[:, :, :, 0:128].reshape(size, 128),
            preferred_element_type=F32,
        ).reshape(4, 128, 128)

        @pl.when(has[f])
        def _():
            halo_copy(r.im0, 1, f).start()

    r.rb2[core, z] = sub_total(r.ra2, 2)
    chips_start(r.rb2, 2)

    for f in range(4):

        @pl.when(has[f])
        def _():
            wait_bytes(halo[1][f], r.hrecv.at[1, f])

    square = jnp.zeros((PAD, 128), F32)
    cross = jnp.zeros((PAD, 128), F32)
    for f in range(4):
        for k in range(4):
            value = r.im0[f, k] - halo[1][f][r.peer[0, 0, 4 * k + f]]
            r.y[f, k] = value
            high, low = split(value)
            r.rhs[k, f, :, 0:128] = high
            r.rhs[k, f, :, 128:256] = low
            square = square + half_on[f] * folded(value * value)
            cross = cross + half_on[f] * folded(value * r.z0[f, k])
    r.ra3[s] = with_rows(
        field_terms(r.d3, r.y), [(6, column_sum(square)), (7, column_sum(cross))]
    )
    sub_start(r.ra3, 3)

    energy = jnp.zeros((PAD, 128), F32)
    for f in range(4):
        pair = jnp.dot(
            r.dual[:, f].reshape(size // 4, size),
            r.rhs[...].reshape(size, 256),
            preferred_element_type=F32,
        )
        part = (pair[:, :128] + pair[:, 128:]).reshape(4, 128, 128)
        energy = energy + folded(r.y[f] * part)
    r.sa[s] = column_sum(energy)
    sub_start(r.sa, 4)

    cores_start(r.rb2, 2)
    cores_end(r.rb2, 2)
    norm_now = at_cluster(r.rb2, 0)[6:7]
    for t in range(1, C):
        norm_now = norm_now + at_cluster(r.rb2, t)[6:7]
    parts = []
    for t in range(C):
        part = at_cluster(r.rb2, t)[PAD : 2 * PAD]
        if t > 0:
            part = part + at_cluster(r.rb2, t - 1)[2 * PAD : 3 * PAD]
        if t < C - 1:
            part = part + at_cluster(r.rb2, t + 1)[0:PAD]
        parts.append(part)
    coarse_image = filled(jnp.concatenate(parts, axis=0))
    shift = solve(coarse_image)
    keep(2, shift)
    shift = filled(shift)
    near_shift = near(2, 0)
    columns = filled(r.cinv[pl.ds(PAD * c, 3 * PAD), :]).T[:, 0 : 3 * PAD]

    total = sub_total(r.ra3, 3)
    answers = jnp.dot(columns, total, precision=HIGHEST)
    tile_rows = lax.broadcasted_iota(jnp.int32, (PAD, 128), 0)
    for t in range(C):
        tile = answers[PAD * t : PAD * (t + 1)]
        r.ub3[t] = jnp.where(tile_rows < 6, tile, total[0:PAD])
    r.rb3[c] = r.ub3[c]
    cluster_start(lambda there: r.ub3.at[there], r.rb3, 3)

    bent = jnp.dot(gfg, shift, precision=HIGHEST)
    overlap = column_sum(coarse_image * shift)
    bent_energy = column_sum(bent * shift)
    shift_energy = 2.0 * column_sum(near_shift * total)

    r.sb[c] = sub_total(r.sa, 4) - shift_energy
    cluster_start(lambda there: r.sb.at[c], r.sb, 4)

    own_inverse = r.cinv[pl.ds(PAD * (c + 1), PAD), :]
    bent_own = jnp.dot(own_inverse, bent, precision=HIGHEST)
    shift_own = near_shift[PAD : 2 * PAD]
    first_own = near(1, 0)[PAD : 2 * PAD]
    weights = packed(near_shift)
    for f in range(4):
        r.y[f] = r.y[f] - spread(weights, f)
    out_w = pltpu.make_async_copy(r.y, r.w_hbm, r.osem.at[2])
    out_w.start()

    total = cluster_total(r.rb3, 3)
    curvature_now = total[7:8]
    length = norm_now / curvature_now
    w_square = total[6:7] - overlap
    w_energy = cluster_total(r.sb, 4) + bent_energy
    norm_next = length * length * w_square - norm_now
    ratio = norm_next / norm_now
    z_energy = curvature_now - 2.0 * length * w_square + length * length * w_energy
    zd_energy = curvature_now - length * w_square
    curvature_next = z_energy + 2.0 * ratio * zd_energy + ratio * ratio * curvature_now
    step = norm_next / curvature_next
    last = (
        first_own
        - length * shift_own
        - step * ((1.0 + ratio) * shift_own - length * (total - bent_own))
    )
    r.last_out[0:PAD] = last
    r.last_out[PAD : PAD + 1] = length + step * (1.0 + ratio)
    r.last_out[PAD + 1 : PAD + 2] = step * length

    for k, buf in enumerate([r.ka, r.ra0, r.ra2, r.ra3, r.sa]):
        wait_bytes(buf.at[pl.ds(0, S - 1)], r.asend.at[k])
    wait_bytes(r.eb.at[pl.ds(0, C - 1)], r.esend)
    for k, buf in ((0, r.kb), (3, r.rb3), (4, r.sb)):
        wait_bytes(buf.at[pl.ds(0, C - 1)], r.bsend.at[k])
    for k, buf in ((1, r.rb0), (2, r.rb2)):
        wait_bytes(buf.at[0, pl.ds(0, Z - 1)], r.bsend.at[k])
        wait_bytes(buf.at[0], r.ksend.at[k])
    for f in range(4):

        @pl.when(has[f])
        def _():
            halo_copy(r.load, 0, f).wait_send()
            halo_copy(r.im0, 1, f).wait_send()
            modes_copy(f).wait_send()

    out_lam.wait()
    out_z0.wait()
    out_w.wait()


def finish(sign, last, lam, z0, w, out, amp_out):
    f = pl.program_id(0)
    grow, back = last[PAD : PAD + 1], last[PAD + 1 : PAD + 2]
    for k in range(4):
        turned = sign[0, 0, 4 * k + f].astype(F32)
        out[k, 0] = turned * (lam[0, k] + grow * z0[0, k] - back * w[0, k])
    amp_out[:, 0] = last[:MODES]


def per_device(C, S, dual_ops, local_load, rigid_modes, coarse_load, gluing_peer, gluing_sign):
    size = dual_ops.shape[-1]
    block = size // 16
    loads = local_load.shape[-1]
    hbm = pl.BlockSpec(memory_space=pltpu.HBM)
    dma = pltpu.SemaphoreType.DMA
    field = pltpu.VMEM((4, 4, block, loads), F32)

    def rows(*shape):
        return pltpu.VMEM((*shape, 128), F32)

    scratch = dict(
        peer=pltpu.SMEM((1, 1, 16), jnp.int32),
        dual=pltpu.VMEM((4, 4, block, size), BF16),
        load=field,
        modes=pltpu.VMEM((MODES, 16, block), F32),
        cload=pltpu.VMEM((MODES, 1, loads), F32),
        lam=field,
        z0=field,
        y=field,
        im0=field,
        rhs=pltpu.VMEM((4, 4, block, 2 * loads), BF16),
        basis=pltpu.VMEM((4, 4, block, 384), BF16),
        t3=pltpu.VMEM((6 * PAD, size), BF16),
        d3=pltpu.VMEM((6 * PAD, size), BF16),
        cinv=rows(PAD * (C + 2)),
        coef=rows(3, PAD * (C + 4)),
        msg=rows(4, block),
        ka=rows(S, PAD),
        kb=rows(C, PAD),
        eb=rows(C, PAD),
        ra0=rows(S, 4 * PAD),
        rb0=rows(2, C // 2, 4 * PAD),
        ra2=rows(S, 3 * PAD),
        rb2=rows(2, C // 2, 3 * PAD),
        ra3=rows(S, 3 * PAD),
        ub3=rows(C, PAD),
        rb3=rows(C, PAD),
        sa=rows(S, 1),
        sb=rows(C, 1),
        lsem=dma((8,)),
        osem=dma((3,)),
        hsend=dma((2, 4)),
        hrecv=dma((2, 4)),
        gsend=dma((4,)),
        grecv=dma((4,)),
        asend=dma((5,)),
        arecv=dma((5,)),
        bsend=dma((5,)),
        brecv=dma((5,)),
        ksend=dma((4,)),
        krecv=dma((4,)),
        esend=dma,
        erecv=dma,
    )
    for f in range(4):
        scratch["h0%d" % f] = rows(4, block)
        scratch["h1%d" % f] = rows(4, block)
        scratch["a%d" % f] = rows(block)
        scratch["r%d" % f] = rows(4, block)
    whole = jax.ShapeDtypeStruct((4, 4, block, loads), F32)
    lam, z0, w, last = pl.pallas_call(
        functools.partial(kernel, C, S),
        out_shape=(whole, whole, whole, jax.ShapeDtypeStruct((2 * PAD, loads), F32)),
        in_specs=[hbm] * 5,
        out_specs=(hbm, hbm, hbm, pl.BlockSpec(memory_space=pltpu.VMEM)),
        scratch_shapes=[scratch[name] for name in NAMES[9:]],
        compiler_params=pltpu.CompilerParams(
            collective_id=0, has_side_effects=True, vmem_limit_bytes=56 * 1024 * 1024
        ),
    )(
        gluing_peer,
        dual_ops.reshape(4, 4, block, size),
        local_load.reshape(4, 4, block, loads),
        rigid_modes.reshape(MODES, 16, block),
        coarse_load.reshape(MODES, 1, loads),
    )
    face = pl.BlockSpec((1, 4, block, loads), lambda f: (f, 0, 0, 0))
    multipliers, amplitudes = pl.pallas_call(
        finish,
        grid=(4,),
        out_shape=(whole, jax.ShapeDtypeStruct((MODES, 1, loads), F32)),
        in_specs=[
            pl.BlockSpec(memory_space=pltpu.SMEM),
            pl.BlockSpec((2 * PAD, loads), lambda f: (0, 0)),
            face,
            face,
            face,
        ],
        out_specs=(
            pl.BlockSpec((4, 1, block, loads), lambda f: (0, f, 0, 0)),
            pl.BlockSpec((MODES, 1, loads), lambda f: (0, 0, 0)),
        ),
    )(gluing_sign, last, lam, z0, w)
    return multipliers.reshape(1, 1, size, loads), amplitudes.reshape(1, MODES, loads)


def solution(mesh):
    return jax.shard_map(
        functools.partial(per_device, mesh.shape["cluster"], mesh.shape["sub"]),
        mesh=mesh,
        in_specs=(
            P("cluster", "sub", None, None),
            P("cluster", "sub", None, None),
            P("cluster", "sub", None, None),
            P("cluster", None, None),
            P("cluster", "sub", None),
            P("cluster", "sub", None),
        ),
        out_specs=(P("cluster", "sub", None, None), P("cluster", None, None)),
        check_vma=False,
    )
```

time: 820 us -> 60.9 us (0.07); the launches traced: 808 us -> 60.7 us
  blocking collectives: 491 us -> 0 us
  local copies, waits for them, and re-layouts: 130 us -> 0 us
  starting transfers between devices: 89.1 us -> 0 us
  Pallas kernels: 0 us -> 60.1 us
  other arithmetic: 54.2 us -> 0 us
  matrix products: 33.3 us -> 0 us
  waiting for transfers between devices: 8.26 us -> 0 us
    psum x7 -> x0, blocking collectives: 371 us -> none  [the longest x2 147 us: project(): lax.psum(jnp.sum(weights * projected * projected, axis=0), ('cluster', 's...]
    all_gather x5 -> x0, blocking collectives: 120 us -> none  [the longest x3 69.8 us: project(): gathered = lax.all_gather(cluster_terms, 'cluster', axis=0, tiled=True)]
    ppermute x32 -> x0, starting transfers between devices: 89.1 us -> none  [passed_along(): lax.ppermute(value, axis, [(source, source + steps) for source in range(l...]
    pallas_call x0 -> x2, Pallas kernels: none -> 60.1 us  [the longest x1 56.3 us: per_device(): pl.pallas_call(functools.partial(kernel, C, S), out_shape=(whole, whole,...]
    unnamed x56 -> x0, local copies, waits for them, and re-layouts: 38.6 us -> none
    another operation x42 -> x0, other arithmetic: 37.7 us -> none  [the longest x36 19.4 us: place(): return jnp.stack(pieces, axis=1).reshape(dual_size, breadth)]
    gather x32 -> x0, local copies, waits for them, and re-layouts: 37 us -> none  [neighbour_parts(): jnp.take(arrived, peer_table[:, facing], axis=0)]
    dot_general x11 -> x0, matrix products: 31.5 us -> none  [the longest x3 21.6 us: dual_images(): images = jnp.dot(operator, signed, preferred_element_type=jnp.float32)]
  transfers between devices with their start and end apart: 32 -> 0, of which waited for: 5 -> 0; matrix products, arithmetic and copies ran while one was open for 11% -> 0% of each run, Pallas kernels for 0% -> 0%
where the time goes in v2:
time: 60.9 us; the launch traced here: 60.7 us
  Pallas kernels  60.1 us (99%)
  between operations  0.64 us (1%)
    pallas_call x1, Pallas kernels, per_device(): pl.pallas_call(functools.partial(kernel, C, S), out_shape=(whole, whole,...  56.3 us
    pallas_call x1, Pallas kernels, per_device(): pl.pallas_call(finish, grid=(4,), out_shape=(whole, jax.ShapeDtypeStruct(...  3.81 us

profile of v2, /device:TPU:1, one launch (start us, length us, event | category | flops | bytes accessed | tf_op | source)
XLA Modules:
  0.0 60.7 jit_solution(3750625780880858325)
XLA Ops:
  0.6 56.3 %shard_map.77 = (f32[4,4,128,128]{3,2,1,0:T(8,128)}, f32[4,4,128,128]{3,2,1,0:T(8,128)}, f32[4,4,128,128]{3,2,1,0:T(8,128)}, f32[16,128]{1,0:T(8,128)}) custom-call(s32[1,1,16]{2,1,0:T(1,128)} %refs_0_.1, bf16[4,4,128,2048]{3,2,1,0:T(8,128)(2,1)} %bitcast.6, f32[4,4,128,128]{3,2,1,0:T(8,128)} %bitcast.7, f32[6,16,128]{2,1,0:T(8,128)} %bitcast.8, ...), custom_call_target="tpu_custom_call" | custom-call | tf_op jit(solution)/shard_map/pallas_call | solution.py:724
  56.9 3.8 %shard_map.78 = (f32[4,4,128,128]{3,2,1,0:T(8,128)}, f32[6,1,128]{2,1,0:T(1,128)}) custom-call(s32[1,1,16]{2,1,0:T(1,128)} %sign.1, f32[16,128]{1,0:T(8,128)} %get-tuple-element.8.last, f32[4,4,128,128]{3,2,1,0:T(8,128)} %get-tuple-element.9.lam, f32[4,4,128,128]{3,2,1,0:T(8,128)} %get-tuple-element.10.z0, f32[4,4,128,128]{3,2,1,0:T(8,128)} %get-tuple-element.11.w), custom_call_target="tpu_custom_call" | custom-call | tf_op jit(solution)/shard_map/pallas_call | solution.py:741

commit v3 on v2

--- a/solution.py
+++ b/solution.py
@@ -123,6 +123,7 @@
     "sa",
     "sb",
     "lsem",
+    "dsem",
     "osem",
     "hsend",
     "hrecv",
@@ -132,6 +133,8 @@
     "arecv",
     "bsend",
     "brecv",
+    "zsend",
+    "zrecv",
     "ksend",
     "krecv",
     "esend",
@@ -154,7 +157,7 @@
 
     cp_modes = pltpu.make_async_copy(r.modes_hbm, r.modes, r.lsem.at[0])
     cp_cload = pltpu.make_async_copy(r.cload_hbm, r.cload, r.lsem.at[1])
-    cp_dual = pltpu.make_async_copy(r.dual_hbm, r.dual, r.lsem.at[2])
+    cp_dual = pltpu.make_async_copy(r.dual_hbm, r.dual, r.dsem)
     cp_load = [
         pltpu.make_async_copy(r.load_hbm.at[:, f], r.load.at[f], r.lsem.at[3 + f]) for f in range(4)
     ]
@@ -213,14 +216,21 @@
     def chips_start(buf, k):
         def body(i, carry):
             there = lax.rem(z + i, Z) * 2 + core
-            send(buf.at[core, z], buf.at[core, z], r.bsend.at[k], r.brecv.at[k], (there, s))
+            send(buf.at[core, z], buf.at[core, z], r.zsend.at[k], r.zrecv.at[k, z], (there, s))
             return carry
 
         lax.fori_loop(1, Z, body, 0)
-
-    def cores_start(buf, k):
-        wait_bytes(buf.at[0, pl.ds(0, Z - 1)], r.brecv.at[k])
-        send(buf.at[core], buf.at[core], r.ksend.at[k], r.krecv.at[k], (2 * z + 1 - core, s))
+        pass_on(buf, k, z)
+
+    def pass_on(buf, k, row):
+        part = buf.at[core, row]
+        send(part, part, r.ksend.at[k], r.krecv.at[k], (2 * z + 1 - core, s))
+
+    def chips_end(buf, k):
+        for i in sorted(range(1, Z), key=lambda i: min(i, Z - i)):
+            row = lax.rem(z + i, Z)
+            wait_bytes(buf.at[core, row], r.zrecv.at[k, row])
+            pass_on(buf, k, row)
 
     def cores_end(buf, k):
         wait_bytes(buf.at[0], r.krecv.at[k])
@@ -233,15 +243,15 @@
 
         lax.fori_loop(1, C, body, 0)
 
+    def cluster_wait(buf, k):
+        wait_bytes(buf.at[pl.ds(0, C - 1)], r.brecv.at[k])
+
     def cluster_total(buf, k):
-        wait_bytes(buf.at[pl.ds(0, C - 1)], r.brecv.at[k])
+        cluster_wait(buf, k)
         total = buf[0]
         for t in range(1, C):
             total = total + buf[t]
         return total
-
-    def at_cluster(buf, t):
-        return buf.at[t % 2, t // 2]
 
     def halo_copy(src, x, f):
         return pltpu.make_async_remote_copy(
@@ -291,7 +301,7 @@
         rows, span, (((1,), (1,)), ((), ())), precision=HIGHEST, preferred_element_type=F32
     )
     coarse_row = jnp.concatenate([coarse_row, jnp.zeros((PAD, 128 - 3 * PAD), F32)], axis=1)
-    r.ka[s] = pltpu.roll(coarse_row, lax.rem(PAD * c + 128 - PAD, 128), 1)
+    coarse_row = pltpu.roll(coarse_row, lax.rem(PAD * c + 128 - PAD, 128), 1)
 
     cp_cload.wait()
     r.eb[c] = jnp.concatenate(
@@ -307,23 +317,29 @@
     ]
     t3_high, t3_low = split(jnp.concatenate(by_face, axis=0))
     r.t3[...] = jnp.concatenate([t3_high, t3_low], axis=0)
-    span_high = span.astype(BF16).astype(F32)
-    gap = jnp.zeros((PAD, size), F32)
-    wide = jnp.concatenate(
-        [span_high, gap, span - span_high, gap, span_high, gap, gap, gap, gap, gap], axis=0
-    )
-    for b in range(16):
-        r.basis[b // 4, b % 4, :, 256:384] = wide[:, 128 * b : 128 * (b + 1)].T.astype(BF16)
-
-    lanes = lax.broadcasted_iota(jnp.int32, (128, 128), 1)
-
-    def tripled(value):
-        high = value.astype(BF16).astype(F32)
-        return (high + pltpu.roll(value - high, 32, 1) + pltpu.roll(high, 64, 1)).astype(BF16)
-
-    cp_dual.wait()
+    def rows_times(left, high, low):
+        pair = jnp.dot(
+            left[...], jnp.concatenate([high, low], axis=1), preferred_element_type=F32
+        )
+        half = 3 * PAD
+        return pair[:half, :128] + (pair[half:, :128] + pair[:half, 128:]) + pair[half:, 128:]
+
+    def field_terms(left, field):
+        return rows_times(left, *split(field[...].reshape(size, 128)))
+
+    for copy in cp_load:
+        copy.wait()
+    load_terms = field_terms(r.t3, r.load)
+    r.ra0[s] = jnp.concatenate(
+        [load_terms[PAD * kind : PAD * kind + MODES] for kind in range(3)] + [coarse_row[0:MODES]],
+        axis=0,
+    )
+
     turned = []
-    for f in range(4):
+
+    def mode_images(f):
+        if f == 0:
+            cp_dual.wait()
         part = jnp.dot(
             r.dual[:, f].reshape(size // 4, size),
             r.basis[:, :, :, 256:384].reshape(size, 128),
@@ -337,58 +353,62 @@
             r.basis[k, f, :, 0:128] = tripled(block)
             side = block if side is None else side + pltpu.roll(block, 32 * k, 1)
         r.msg[f] = side
+
+    pl.semaphore_wait(barrier, S - 1 + C - 1)
+    sub_start(r.ra0, 1)
+
+    def send_e(i, carry):
+        send(r.eb.at[c], r.eb.at[c], r.esend, r.erecv, (lax.rem(c + i, C), s))
+        return carry
+
+    lax.fori_loop(1, C, send_e, 0)
+
+    span_high = span.astype(BF16).astype(F32)
+    gap = jnp.zeros((PAD, size), F32)
+    wide = jnp.concatenate(
+        [span_high, gap, span - span_high, gap, span_high, gap, gap, gap, gap, gap], axis=0
+    )
+    for b in range(16):
+        r.basis[b // 4, b % 4, :, 256:384] = wide[:, 128 * b : 128 * (b + 1)].T.astype(BF16)
+
+    lanes = lax.broadcasted_iota(jnp.int32, (128, 128), 1)
+
+    def tripled(value):
+        high = value.astype(BF16).astype(F32)
+        return (high + pltpu.roll(value - high, 32, 1) + pltpu.roll(high, 64, 1)).astype(BF16)
+
+    for f in range(4):
+        mode_images(f)
     d3_high, d3_low = split(jnp.concatenate(turned, axis=1))
     r.d3[...] = jnp.concatenate([d3_high, d3_low], axis=0)
-
-    def rows_times(left, high, low):
-        pair = jnp.dot(
-            left[...], jnp.concatenate([high, low], axis=1), preferred_element_type=F32
-        )
-        half = 3 * PAD
-        return pair[:half, :128] + (pair[half:, :128] + pair[:half, 128:]) + pair[half:, 128:]
-
-    def field_terms(left, field):
-        return rows_times(left, *split(field[...].reshape(size, 128)))
-
-    for copy in cp_load:
-        copy.wait()
     mode_terms = field_terms(r.t3, r.im0)
-    r.ra0[s, 0 : 3 * PAD] = field_terms(r.t3, r.load)
-    r.ra0[s, 3 * PAD : 4 * PAD] = (
+    r.ka[s] = (
         mode_terms[0:PAD]
         + pltpu.roll(mode_terms[PAD : 2 * PAD], 32, 1)
         + pltpu.roll(mode_terms[2 * PAD : 3 * PAD], 64, 1)
     )
-
-    pl.semaphore_wait(barrier, S - 1 + C - 1)
     sub_start(r.ka, 0)
-    sub_start(r.ra0, 1)
-
-    def send_e(i, carry):
-        send(r.eb.at[c], r.eb.at[c], r.esend, r.erecv, (lax.rem(c + i, C), s))
-        return carry
-
-    lax.fori_loop(1, C, send_e, 0)
+    r.rb0[core, z] = sub_total(r.ra0, 1)
+    chips_start(r.rb0, 0)
+    r.kb[c] = sub_total(r.ka, 0)
+    cluster_start(lambda there: r.kb.at[c], r.kb, 0)
 
     for f in range(4):
 
         @pl.when(has[f])
         def _():
             halo_copy(r.load, 0, f).start()
-
-    r.kb[c] = sub_total(r.ka, 0)
-    cluster_start(lambda there: r.kb.at[c], r.kb, 0)
-    r.rb0[core, z] = sub_total(r.ra0, 1)
-    chips_start(r.rb0, 1)
-    for f in range(4):
-
-        @pl.when(has[f])
-        def _():
             modes_copy(f).start()
 
-    cores_start(r.rb0, 1)
-    wait_bytes(r.kb.at[pl.ds(0, C - 1)], r.brecv.at[0])
-    inverse = coarse_inverse([r.kb[t] for t in range(C)])
+    chips_end(r.rb0, 0)
+    cores_end(r.rb0, 0)
+    blank = jnp.zeros((PAD - MODES, 128), F32)
+    inverse = coarse_inverse(
+        [
+            jnp.concatenate([r.rb0[t % 2, t // 2, 3 * MODES : 4 * MODES], blank], axis=0)
+            for t in range(C)
+        ]
+    )
     zero_tile = jnp.zeros((PAD, 128), F32)
     r.cinv[0:PAD] = zero_tile
     for t in range(C):
@@ -463,23 +483,23 @@
                 part = part - tile(t - 1, 2)
             if t < C - 1:
                 part = part - tile(t + 1, 1)
-            parts.append(part)
+            parts += [part, blank]
         return filled(jnp.concatenate(parts, axis=0))
 
-    def term(buf):
-        return lambda t, kind: at_cluster(buf, t)[PAD * kind : PAD * (kind + 1)]
-
-    tile_lanes = lax.broadcasted_iota(jnp.int32, (PAD, 128), 1)
+    def load_term(t, kind):
+        return r.rb0[t % 2, t // 2, MODES * kind : MODES * (kind + 1)]
+
+    tile_lanes = lax.broadcasted_iota(jnp.int32, (MODES, 128), 1)
 
     def mode_term(t, kind):
-        value = at_cluster(r.rb0, t)[3 * PAD : 4 * PAD]
+        value = r.kb[t, 0:MODES]
         value = jnp.where((tile_lanes >= 32 * kind) & (tile_lanes < 32 * kind + 3 * PAD), value, 0.0)
         turn = (PAD * (t - 1) - 32 * kind) % 128
         return pltpu.roll(value, turn, 1) if turn else value
 
-    cores_end(r.rb0, 1)
+    cluster_wait(r.kb, 0)
     gfg = joined(mode_term)
-    coarse_now = joined(term(r.rb0)) - jnp.dot(gfg, start, precision=HIGHEST)
+    coarse_now = joined(load_term) - jnp.dot(gfg, start, precision=HIGHEST)
     first = solve(coarse_now)
     keep(1, first)
     weights = packed(near(1, 0))
@@ -526,8 +546,10 @@
         def _():
             halo_copy(r.im0, 1, f).start()
 
+    columns = filled(r.cinv[pl.ds(PAD * c, 3 * PAD), :]).T[:, 0 : 3 * PAD]
+    own_inverse = r.cinv[pl.ds(PAD * (c + 1), PAD), :]
     r.rb2[core, z] = sub_total(r.ra2, 2)
-    chips_start(r.rb2, 2)
+    chips_start(r.rb2, 1)
 
     for f in range(4):
 
@@ -560,28 +582,28 @@
         )
         part = (pair[:, :128] + pair[:, 128:]).reshape(4, 128, 128)
         energy = energy + folded(r.y[f] * part)
+        if f == 1:
+            chips_end(r.rb2, 1)
     r.sa[s] = column_sum(energy)
     sub_start(r.sa, 4)
 
-    cores_start(r.rb2, 2)
-    cores_end(r.rb2, 2)
-    norm_now = at_cluster(r.rb2, 0)[6:7]
+    cores_end(r.rb2, 1)
+    norm_now = r.rb2[0, 0, 6:7]
     for t in range(1, C):
-        norm_now = norm_now + at_cluster(r.rb2, t)[6:7]
+        norm_now = norm_now + r.rb2[t % 2, t // 2, 6:7]
     parts = []
     for t in range(C):
-        part = at_cluster(r.rb2, t)[PAD : 2 * PAD]
+        part = r.rb2[t % 2, t // 2, PAD : 2 * PAD]
         if t > 0:
-            part = part + at_cluster(r.rb2, t - 1)[2 * PAD : 3 * PAD]
+            part = part + r.rb2[(t - 1) % 2, (t - 1) // 2, 2 * PAD : 3 * PAD]
         if t < C - 1:
-            part = part + at_cluster(r.rb2, t + 1)[0:PAD]
+            part = part + r.rb2[(t + 1) % 2, (t + 1) // 2, 0:PAD]
         parts.append(part)
     coarse_image = filled(jnp.concatenate(parts, axis=0))
     shift = solve(coarse_image)
     keep(2, shift)
     shift = filled(shift)
     near_shift = near(2, 0)
-    columns = filled(r.cinv[pl.ds(PAD * c, 3 * PAD), :]).T[:, 0 : 3 * PAD]
 
     total = sub_total(r.ra3, 3)
     answers = jnp.dot(columns, total, precision=HIGHEST)
@@ -600,7 +622,6 @@
     r.sb[c] = sub_total(r.sa, 4) - shift_energy
     cluster_start(lambda there: r.sb.at[c], r.sb, 4)
 
-    own_inverse = r.cinv[pl.ds(PAD * (c + 1), PAD), :]
     bent_own = jnp.dot(own_inverse, bent, precision=HIGHEST)
     shift_own = near_shift[PAD : 2 * PAD]
     first_own = near(1, 0)[PAD : 2 * PAD]
@@ -633,11 +654,11 @@
     for k, buf in enumerate([r.ka, r.ra0, r.ra2, r.ra3, r.sa]):
         wait_bytes(buf.at[pl.ds(0, S - 1)], r.asend.at[k])
     wait_bytes(r.eb.at[pl.ds(0, C - 1)], r.esend)
+    for k, buf in enumerate([r.rb0, r.rb2]):
+        wait_bytes(buf.at[0, pl.ds(0, Z - 1)], r.zsend.at[k])
+        wait_bytes(buf.at[0], r.ksend.at[k])
     for k, buf in ((0, r.kb), (3, r.rb3), (4, r.sb)):
         wait_bytes(buf.at[pl.ds(0, C - 1)], r.bsend.at[k])
-    for k, buf in ((1, r.rb0), (2, r.rb2)):
-        wait_bytes(buf.at[0, pl.ds(0, Z - 1)], r.bsend.at[k])
-        wait_bytes(buf.at[0], r.ksend.at[k])
     for f in range(4):
 
         @pl.when(has[f])
@@ -651,13 +672,36 @@
     out_w.wait()
 
 
-def finish(sign, last, lam, z0, w, out, amp_out):
-    f = pl.program_id(0)
+def finish(sign, last_hbm, lam_hbm, z0_hbm, w_hbm, out_hbm, amp_hbm, last, lam, z0, w, amp, sems):
+    cp_last = pltpu.make_async_copy(last_hbm, last, sems.at[4, 0])
+    cp_last.start()
+    copies = [
+        [
+            pltpu.make_async_copy(src.at[f], dst.at[f], sems.at[f, i])
+            for i, (src, dst) in enumerate(((lam_hbm, lam), (z0_hbm, z0), (w_hbm, w)))
+        ]
+        for f in range(4)
+    ]
+    for group in copies:
+        for copy in group:
+            copy.start()
+    cp_last.wait()
     grow, back = last[PAD : PAD + 1], last[PAD + 1 : PAD + 2]
-    for k in range(4):
-        turned = sign[0, 0, 4 * k + f].astype(F32)
-        out[k, 0] = turned * (lam[0, k] + grow * z0[0, k] - back * w[0, k])
-    amp_out[:, 0] = last[:MODES]
+    amp[:, 0] = last[:MODES]
+    results = [pltpu.make_async_copy(amp, amp_hbm, sems.at[4, 1])]
+    results[0].start()
+    for f in range(4):
+        for copy in copies[f]:
+            copy.wait()
+        for k in range(4):
+            turned = sign[0, 0, 4 * k + f].astype(F32)
+            lam[f, k] = turned * (lam[f, k] + grow * z0[f, k] - back * w[f, k])
+        for k in range(4):
+            result = pltpu.make_async_copy(lam.at[f, k], out_hbm.at[k, f], sems.at[5 + f, k])
+            result.start()
+            results.append(result)
+    for result in results:
+        result.wait()
 
 
 def per_device(C, S, dual_ops, local_load, rigid_modes, coarse_load, gluing_peer, gluing_sign):
@@ -691,8 +735,8 @@
         ka=rows(S, PAD),
         kb=rows(C, PAD),
         eb=rows(C, PAD),
-        ra0=rows(S, 4 * PAD),
-        rb0=rows(2, C // 2, 4 * PAD),
+        ra0=rows(S, 4 * MODES),
+        rb0=rows(2, C // 2, 4 * MODES),
         ra2=rows(S, 3 * PAD),
         rb2=rows(2, C // 2, 3 * PAD),
         ra3=rows(S, 3 * PAD),
@@ -701,6 +745,7 @@
         sa=rows(S, 1),
         sb=rows(C, 1),
         lsem=dma((8,)),
+        dsem=dma,
         osem=dma((3,)),
         hsend=dma((2, 4)),
         hrecv=dma((2, 4)),
@@ -710,8 +755,10 @@
         arecv=dma((5,)),
         bsend=dma((5,)),
         brecv=dma((5,)),
-        ksend=dma((4,)),
-        krecv=dma((4,)),
+        zsend=dma((2,)),
+        zrecv=dma((2, C // 2)),
+        ksend=dma((2,)),
+        krecv=dma((2,)),
         esend=dma,
         erecv=dma,
     )
@@ -737,22 +784,19 @@
         rigid_modes.reshape(MODES, 16, block),
         coarse_load.reshape(MODES, 1, loads),
     )
-    face = pl.BlockSpec((1, 4, block, loads), lambda f: (f, 0, 0, 0))
     multipliers, amplitudes = pl.pallas_call(
         finish,
-        grid=(4,),
         out_shape=(whole, jax.ShapeDtypeStruct((MODES, 1, loads), F32)),
-        in_specs=[
-            pl.BlockSpec(memory_space=pltpu.SMEM),
-            pl.BlockSpec((2 * PAD, loads), lambda f: (0, 0)),
-            face,
-            face,
-            face,
+        in_specs=[pl.BlockSpec(memory_space=pltpu.SMEM)] + [hbm] * 4,
+        out_specs=(hbm, hbm),
+        scratch_shapes=[
+            rows(2 * PAD),
+            field,
+            field,
+            field,
+            pltpu.VMEM((MODES, 1, loads), F32),
+            dma((9, 4)),
         ],
-        out_specs=(
-            pl.BlockSpec((4, 1, block, loads), lambda f: (0, f, 0, 0)),
-            pl.BlockSpec((MODES, 1, loads), lambda f: (0, 0, 0)),
-        ),
     )(gluing_sign, last, lam, z0, w)
     return multipliers.reshape(1, 1, size, loads), amplitudes.reshape(1, MODES, loads)
 

time: 60.9 us -> 58.1 us (0.954)
  Pallas kernels: 60.1 us -> 57.3 us
    pallas_call x1, Pallas kernels: 56.3 us -> 53.8 us  [per_device(): pl.pallas_call(functools.partial(kernel, C, S), out_shape=(whole, whole,...]
where the time goes in v3:
time: 58.1 us; the launch traced here: 58 us
  Pallas kernels  57.3 us (99%)
  between operations  0.64 us (1%)
    pallas_call x1, Pallas kernels, per_device(): pl.pallas_call(functools.partial(kernel, C, S), out_shape=(whole, whole,...  53.8 us
    pallas_call x1, Pallas kernels, per_device(): pl.pallas_call(finish, out_shape=(whole, jax.ShapeDtypeStruct((MODES, 1,...  3.56 us

profile of v3, /device:TPU:1, one launch (start us, length us, event | category | flops | bytes accessed | tf_op | source)
XLA Modules:
  0.0 58.0 jit_solution(14451576190895487594)
XLA Ops:
  0.6 53.8 %shard_map.77 = (f32[4,4,128,128]{3,2,1,0:T(8,128)}, f32[4,4,128,128]{3,2,1,0:T(8,128)}, f32[4,4,128,128]{3,2,1,0:T(8,128)}, f32[16,128]{1,0:T(8,128)}) custom-call(s32[1,1,16]{2,1,0:T(1,128)} %refs_0_.1, bf16[4,4,128,2048]{3,2,1,0:T(8,128)(2,1)} %bitcast.6, f32[4,4,128,128]{3,2,1,0:T(8,128)} %bitcast.7, f32[6,16,128]{2,1,0:T(8,128)} %bitcast.8, ...), custom_call_target="tpu_custom_call" | custom-call | tf_op jit(solution)/shard_map/pallas_call | solution.py:771
  54.4 3.6 %shard_map.78 = (f32[4,4,128,128]{3,2,1,0:T(8,128)}, f32[6,1,128]{2,1,0:T(1,128)}) custom-call(s32[1,1,16]{2,1,0:T(1,128)} %sign.1, f32[16,128]{1,0:T(8,128)} %get-tuple-element.8.last_hbm, f32[4,4,128,128]{3,2,1,0:T(8,128)} %get-tuple-element.9.lam_hbm, f32[4,4,128,128]{3,2,1,0:T(8,128)} %get-tuple-element.10.z0_hbm, f32[4,4,128,128]{3,2,1,0:T(8,128)} %get-tuple-element.11.w_hbm), custom_call_target="tpu_custom_call" | custom-call | tf_op jit(solution)/shard_map/pallas_call | solution.py:787

commit v4 on v3

--- a/solution.py
+++ b/solution.py
@@ -390,15 +390,15 @@
     sub_start(r.ka, 0)
     r.rb0[core, z] = sub_total(r.ra0, 1)
     chips_start(r.rb0, 0)
-    r.kb[c] = sub_total(r.ka, 0)
-    cluster_start(lambda there: r.kb.at[c], r.kb, 0)
-
     for f in range(4):
 
         @pl.when(has[f])
         def _():
             halo_copy(r.load, 0, f).start()
             modes_copy(f).start()
+
+    r.kb[c] = sub_total(r.ka, 0)
+    cluster_start(lambda there: r.kb.at[c], r.kb, 0)
 
     chips_end(r.rb0, 0)
     cores_end(r.rb0, 0)

time: 58.1 us -> 57.3 us (0.986)
  Pallas kernels: 57.3 us -> 56.5 us
    pallas_call x1, Pallas kernels: 53.8 us -> 52.9 us  [per_device(): pl.pallas_call(functools.partial(kernel, C, S), out_shape=(whole, whole,...]
where the time goes in v4:
time: 57.3 us; the launch traced here: 57.1 us
  Pallas kernels  56.5 us (99%)
  between operations  0.64 us (1%)
    pallas_call x1, Pallas kernels, per_device(): pl.pallas_call(functools.partial(kernel, C, S), out_shape=(whole, whole,...  52.9 us
    pallas_call x1, Pallas kernels, per_device(): pl.pallas_call(finish, out_shape=(whole, jax.ShapeDtypeStruct((MODES, 1,...  3.56 us

profile of v4, /device:TPU:1, one launch (start us, length us, event | category | flops | bytes accessed | tf_op | source)
XLA Modules:
  0.0 57.1 jit_solution(16324330992212264924)
XLA Ops:
  0.6 52.9 %shard_map.77 = (f32[4,4,128,128]{3,2,1,0:T(8,128)}, f32[4,4,128,128]{3,2,1,0:T(8,128)}, f32[4,4,128,128]{3,2,1,0:T(8,128)}, f32[16,128]{1,0:T(8,128)}) custom-call(s32[1,1,16]{2,1,0:T(1,128)} %refs_0_.1, bf16[4,4,128,2048]{3,2,1,0:T(8,128)(2,1)} %bitcast.6, f32[4,4,128,128]{3,2,1,0:T(8,128)} %bitcast.7, f32[6,16,128]{2,1,0:T(8,128)} %bitcast.8, ...), custom_call_target="tpu_custom_call" | custom-call | tf_op jit(solution)/shard_map/pallas_call | solution.py:771
  53.5 3.6 %shard_map.78 = (f32[4,4,128,128]{3,2,1,0:T(8,128)}, f32[6,1,128]{2,1,0:T(1,128)}) custom-call(s32[1,1,16]{2,1,0:T(1,128)} %sign.1, f32[16,128]{1,0:T(8,128)} %get-tuple-element.8.last_hbm, f32[4,4,128,128]{3,2,1,0:T(8,128)} %get-tuple-element.9.lam_hbm, f32[4,4,128,128]{3,2,1,0:T(8,128)} %get-tuple-element.10.z0_hbm, f32[4,4,128,128]{3,2,1,0:T(8,128)} %get-tuple-element.11.w_hbm), custom_call_target="tpu_custom_call" | custom-call | tf_op jit(solution)/shard_map/pallas_call | solution.py:787
